TPU v7x, 256 devices: a whole 4x4x8 slice. The times are simulated.
256 devices in a mesh: lat: 8 (over y, x_lo), lon: 32 (over x_hi, z, core).
Axes of the slice: x: 4 (x_hi: 2, x_lo: 2; x = x_hi * 2 + x_lo), y: 4, z: 8, core: 2. Of those that a mesh axis runs over, the one named last changes fastest.
Arguments:
- coarse_field: bfloat16 [1, 128, 256, 2048], P(None, None, 'lat', 'lon'), may hold values from -6 to 6
- cotangent: bfloat16 [1, 64, 512, 4096], P(None, None, 'lat', 'lon'), may hold values from -6 to 6
- tconv_weight: bfloat16 [4, 64, 128], replicated, may hold values from -0.5 to 0.5
- conv_weight: bfloat16 [64, 576], replicated, may hold values from -0.25 to 0.25
Outputs:
- coarse_grad: bfloat16 [1, 128, 256, 2048], P(None, None, 'lat', 'lon')
- tconv_grad: float32 [4, 64, 128], replicated
- conv_grad: float32 [64, 576], replicated
All inputs are finite; a program needn't handle non-finite values.
Results may differ from a plain program's by a relative error of at most 0.0049.
Values may be sent and summed in bfloat16 or wider, within the bound.
A program may use at most 128 MiB of HBM per device.

v0:
```python
import functools
import math

import jax
import jax.numpy as jnp
from jax import lax
from jax.experimental import pallas as pl
from jax.experimental.pallas import tpu as pltpu
from jax.sharding import PartitionSpec as P

MESH = pl.DeviceIdType.MESH
F32, BF16 = jnp.float32, jnp.bfloat16
OWN, BESIDE = 0, 1


def row_step(source, half, p):
    step = p - half if source == OWN else (p - 2 if half == 0 else p + 1)
    return step if abs(step) <= 1 else None


def col_step(window, q):
    step = (q, q - 1, q + 1, q - 2)[window]
    return step if abs(step) <= 1 else None


def window_blocks():
    for source in (OWN, BESIDE):
        for window in range(4):
            for half in range(2):
                for p in range(2):
                    for q in range(2):
                        a, b = row_step(source, half, p), col_step(window, q)
                        if a is not None and b is not None:
                            yield source, window, half, p, q, 3 * (a + 1) + b + 1


def pole_blocks():
    for window in range(4):
        for half in range(2):
            for q in range(2):
                b = col_step(window, q)
                if b is not None:
                    yield window, half, half, q, 3 * (2 * half) + b + 1


def across(a, b):
    return lax.dot_general(a, b, (((1,), (1,)), ((), ())), preferred_element_type=F32)


def times(a, b):
    return jnp.dot(a, b, preferred_element_type=F32)


def section_kernel(
    coarse_ref, cot_ref, tconv_ref, conv_ref, out_ref, sums_ref,
    spread, tiles, west_out, east_out, west_in, east_in, patches, act_t, slope, pre_t, weights, pole_weights,
    pole_patches, pole_extra, pole_sums, send_sem, recv_sem,
):
    pairs = coarse_ref.shape[0] // 64
    chunks = pairs // 4
    lat, lon = lax.axis_index("lat"), lax.axis_index("lon")
    lats, lons = lax.axis_size("lat"), lax.axis_size("lon")
    at_north, at_south = lat == 0, lat == lats - 1
    opposite = lax.rem(lon + lons // 2, lons)
    up_lat, up_lon = jnp.where(at_north, 0, lat - 1), jnp.where(at_north, opposite, lon)
    down_lat, down_lon = jnp.where(at_south, lats - 1, lat + 1), jnp.where(at_south, opposite, lon)

    def beside(which_lat, which_lon, by):
        return {"lat": which_lat, "lon": lax.rem(which_lon + by + lons, lons)}

    barrier = pltpu.get_barrier_semaphore()
    for which in ((lat, lon, -1), (lat, lon, 1), (up_lat, up_lon, -1), (up_lat, up_lon, 0), (up_lat, up_lon, 1),
                  (down_lat, down_lon, -1), (down_lat, down_lon, 0), (down_lat, down_lon, 1)):
        pl.semaphore_signal(barrier, inc=1, device_id=beside(*which), device_id_type=MESH)

    rows, cols = lax.broadcasted_iota(jnp.int32, (128, 128), 0), lax.broadcasted_iota(jnp.int32, (128, 128), 1)
    order = jnp.where(rows == (cols % 64) * 2 + cols // 64, 1.0, 0.0).astype(BF16)
    height = 2 * pairs

    def reorder(n, carry):
        at = pl.ds(pl.multiple_of(n * 512, 512), 512)
        spread[at, :] = times(cot_ref[at, :], order)
        return carry

    lax.fori_loop(0, 64 * height // 512, reorder, 0)

    def make_tile(i, carry):
        pair = jnp.concatenate(
            [spread[pl.ds(2 * i, 64, stride=height), :], spread[pl.ds(2 * i + 1, 64, stride=height), :]], axis=0)
        tile = pair.T
        tiles[i + 1, 0] = tile[:64].astype(BF16)
        tiles[i + 1, 1] = tile[64:].astype(BF16)
        west_out[pl.ds(i, 1), :] = tile[:1]
        east_out[pl.ds(i, 1), :] = tile[127:]
        return carry

    lax.fori_loop(0, pairs, make_tile, 0, unroll=2)

    pl.semaphore_wait(barrier, 8)
    copies = []

    def send(source, target, sem, which, landed):
        copy = pltpu.make_async_remote_copy(
            src_ref=source, dst_ref=target, send_sem=send_sem.at[sem], recv_sem=recv_sem.at[landed],
            device_id=beside(*which), device_id_type=MESH)
        copy.start()
        copies.append(copy)

    head, tail = pl.ds(0, 8), pl.ds(pairs - 8, 8)
    up_slot = jnp.where(at_north, 0, pairs + 1)
    down_slot = jnp.where(at_south, pairs + 1, 0)
    up_corner = pl.ds(pl.multiple_of(jnp.where(at_north, 0, pairs + 8), 8), 8)
    down_corner = pl.ds(pl.multiple_of(jnp.where(at_south, pairs + 8, 0), 8), 8)
    up_sem, down_sem = jnp.where(at_north, 0, 1), jnp.where(at_south, 1, 0)
    send(west_out, east_in.at[pl.ds(8, pairs)], 0, (lat, lon, -1), 6)
    send(east_out, west_in.at[pl.ds(8, pairs)], 1, (lat, lon, 1), 7)
    send(tiles.at[1, pl.ds(0, 2)], tiles.at[up_slot, pl.ds(0, 2)], 2, (up_lat, up_lon, 0), up_sem)
    send(tiles.at[pairs, pl.ds(0, 2)], tiles.at[down_slot, pl.ds(0, 2)], 3, (down_lat, down_lon, 0), down_sem)
    send(west_out.at[head], east_in.at[up_corner], 4, (up_lat, up_lon, -1), 2 + up_sem)
    send(east_out.at[head], west_in.at[up_corner], 5, (up_lat, up_lon, 1), 4 + up_sem)
    send(west_out.at[tail], east_in.at[down_corner], 6, (down_lat, down_lon, -1), 2 + down_sem)
    send(east_out.at[tail], west_in.at[down_corner], 7, (down_lat, down_lon, 1), 4 + down_sem)

    def activate(n, carry):
        at = pl.ds(pl.multiple_of(n * 256, 256), 256)
        up = across(coarse_ref[at, :], tconv_ref[...])
        logistic = 0.5 * jnp.tanh(0.5 * up) + 0.5
        act_t[:, at] = (up * logistic).astype(BF16).T
        slope[at, :] = logistic * (1.0 + up * (1.0 - logistic))
        return carry

    lax.fori_loop(0, chunks, activate, 0)

    def block(tap):
        return conv_ref[:, 64 * tap : 64 * tap + 64]

    none = jnp.zeros((64, 64), BF16)
    places = {(s, w, h, p, q): t for s, w, h, p, q, t in window_blocks()}
    for s, w, h in [(s, w, h) for s in range(2) for w in range(4) for h in range(2)]:
        line = [block(places[s, w, h, p, q]) if (s, w, h, p, q) in places else none for p in range(2) for q in range(2)]
        at = w * 256 + s * 128 + h * 64
        weights[at : at + 64, :] = jnp.concatenate(line, axis=1)
    places = {(w, h, p, q): t for w, h, p, q, t in pole_blocks()}
    for w, h in [(w, h) for w in range(4) for h in range(2)]:
        line = [block(places[w, h, p, q]) if (w, h, p, q) in places else none for p in range(2) for q in range(2)]
        at = w * 128 + h * 64
        pole_weights[at : at + 64, :] = jnp.concatenate(line, axis=1)

    pole_extra[...] = jnp.zeros_like(pole_extra)
    pole_sums[...] = jnp.zeros_like(pole_sums)

    for landed, source in enumerate(
        (tiles.at[0, pl.ds(0, 2)], tiles.at[0, pl.ds(0, 2)], east_in.at[head], east_in.at[head], west_in.at[head],
         west_in.at[head], east_in.at[pl.ds(8, pairs)], west_in.at[pl.ds(8, pairs)])):
        pltpu.make_async_remote_copy(
            src_ref=source, dst_ref=source, send_sem=send_sem.at[0], recv_sem=recv_sem.at[landed],
            device_id=beside(lat, lon, 1), device_id_type=MESH).wait_recv()

    line = lax.broadcasted_iota(jnp.int32, (64, 128), 0)

    def shift(i, west_row, east_row):
        even, odd = tiles[i, 0].astype(F32), tiles[i, 1].astype(F32)
        tiles[i, 2] = jnp.where(line == 0, west_in[pl.ds(west_row, 1), :], pltpu.roll(odd, 1, 0)).astype(BF16)
        tiles[i, 3] = jnp.where(line == 63, east_in[pl.ds(east_row, 1), :], pltpu.roll(even, 63, 0)).astype(BF16)

    def shift_own(i, carry):
        shift(i, i + 7, i + 7)
        return carry

    north_row, south_row = jnp.where(at_north, 0, 7), jnp.where(at_south, pairs + 15, pairs + 8)
    shift(0, north_row, north_row)
    shift(pairs + 1, south_row, south_row)
    lax.fori_loop(1, pairs + 1, shift_own, 0, unroll=2)

    lane = lax.broadcasted_iota(jnp.int32, (64, 128), 1)
    blank = jnp.zeros((64, 128), BF16)

    def take_pole(slot, first, keep):
        for w in range(4):
            pole_patches[first : first + 64, 128 * w : 128 * w + 128] = jnp.where(keep, tiles[slot, w].astype(F32), 0.0).astype(BF16)
            pole_patches[64 - first : 128 - first, 128 * w : 128 * w + 128] = blank
            tiles[slot, w] = blank

    last = pairs * 64

    @pl.when(at_north)
    def _():
        take_pole(0, 0, lane < 64)
        pole_extra[0] = times(pole_patches[...], pole_weights[...])
        pole_sums[...] = times(act_t[:, :128], pole_patches[...])

    @pl.when(at_south)
    def _():
        take_pole(pairs + 1, 64, lane >= 64)
        pole_extra[1] = times(pole_patches[...], pole_weights[...])
        pole_sums[...] = times(act_t[:, last - 128 :], pole_patches[...])

    def lay(i, carry):
        at = pl.ds(pl.multiple_of(i * 64, 64), 64)
        for w in range(4):
            patches[at, 256 * w : 256 * w + 128] = tiles[i + 1, w]
            patches[at, 256 * w + 128 : 256 * w + 256] = jnp.where(lane < 64, tiles[i + 2, w], tiles[i, w])
        return carry

    lax.fori_loop(0, pairs, lay, 0, unroll=2)

    found = {}

    def add(tap, value):
        found[tap] = value if tap not in found else found[tap] + value

    for w in range(4):
        grads = times(act_t[...], patches[:, 256 * w : 256 * w + 256])
        for s, ww, h, p, q, t in window_blocks():
            if ww == w:
                at, col = 128 * p + 64 * q, s * 128 + h * 64
                add(t, grads[at : at + 64, col : col + 64])
    for w, h, p, q, t in pole_blocks():
        at, col = 128 * p + 64 * q, w * 128 + h * 64
        add(t, pole_sums[at : at + 64, col : col + 64])
    for m in range(5):
        both = jnp.concatenate([found[2 * m], found[2 * m + 1] if m < 4 else jnp.zeros((64, 64), F32)], axis=0)
        sums_ref[64 * m : 64 * m + 64, :] = both.T

    for n in range(chunks):
        at = slice(n * 256, n * 256 + 256)
        grad = times(patches[at, :], weights[...])
        if n == 0:
            grad = jnp.concatenate([grad[:128] + pole_extra[0], grad[128:]], axis=0)
        if n == chunks - 1:
            grad = jnp.concatenate([grad[:128], grad[128:] + pole_extra[1]], axis=0)
        pre = (grad * slope[at, :]).astype(BF16)
        pre_t[:, at] = pre.T
        out_ref[at, :] = times(pre, tconv_ref[...]).astype(BF16)
    sums_ref[320:576, :] = times(pre_t[...], coarse_ref[...])
    sums_ref[576:, :] = jnp.zeros((64, 128), F32)

    for copy in copies:
        copy.wait_send()


def section(coarse, cotangent, tconv, conv):
    cells = coarse.shape[0]
    pairs = cells // 64
    vmem = pl.BlockSpec(memory_space=pltpu.VMEM)
    return pl.pallas_call(
        section_kernel,
        out_shape=(jax.ShapeDtypeStruct((cells, 128), BF16), jax.ShapeDtypeStruct((ROWS, 128), F32)),
        in_specs=[vmem] * 4,
        out_specs=(vmem, vmem),
        scratch_shapes=[
            pltpu.VMEM((cells * 2, 128), F32),
            pltpu.VMEM((pairs + 2, 4, 64, 128), BF16),
            pltpu.VMEM((pairs, 128), F32), pltpu.VMEM((pairs, 128), F32),
            pltpu.VMEM((pairs + 16, 128), F32), pltpu.VMEM((pairs + 16, 128), F32),
            pltpu.VMEM((cells, 1024), BF16),
            pltpu.VMEM((256, cells), BF16),
            pltpu.VMEM((cells, 256), F32),
            pltpu.VMEM((256, cells), BF16),
            pltpu.VMEM((1024, 256), BF16),
            pltpu.VMEM((512, 256), BF16),
            pltpu.VMEM((128, 512), BF16),
            pltpu.VMEM((2, 128, 256), F32),
            pltpu.VMEM((256, 512), F32),
            pltpu.SemaphoreType.DMA((8,)), pltpu.SemaphoreType.DMA((8,)),
        ],
        compiler_params=pltpu.CompilerParams(collective_id=0, has_side_effects=True, vmem_limit_bytes=40 * 2**20),
        name="section",
    )(coarse, cotangent, tconv, conv)


ROWS = 640
PART = 40


def sum_kernel(scale, x_ref, o_ref, seen, part, slots, done, a_send, a_recv, b_send, b_recv, c_send, c_recv, d_send, d_recv):
    lat, lon = lax.axis_index("lat"), lax.axis_index("lon")
    far, near = lon // 16, lon % 16
    mine = far * 8 + lat

    def plane(member):
        return {"lat": member % 8, "lon": (member // 8) * 16 + near}

    def line(member):
        return {"lat": lat, "lon": far * 16 + member}

    barrier = pltpu.get_barrier_semaphore()
    for d in range(1, 16):
        pl.semaphore_signal(barrier, inc=1, device_id=plane((mine + d) % 16), device_id_type=MESH)
        pl.semaphore_signal(barrier, inc=1, device_id=line((near + d) % 16), device_id_type=MESH)
    pl.semaphore_wait(barrier, 30)

    def rows_of(member):
        return pl.ds(pl.multiple_of(member * PART, 8), PART)

    firsts = []
    for d in range(1, 16):
        peer = (mine + d) % 16
        copy = pltpu.make_async_remote_copy(
            src_ref=x_ref.at[rows_of(peer)], dst_ref=seen.at[d], send_sem=a_send.at[d], recv_sem=a_recv.at[d],
            device_id=plane(peer), device_id_type=MESH)
        copy.start()
        firsts.append(copy)
    total = x_ref[rows_of(mine), :]
    for d in range(1, 16):
        firsts[d - 1].wait_recv()
        total = total + seen[d]
    part[...] = total

    for k in range(5):
        owner = 3 * k

        def send(k=k, owner=owner):
            pltpu.make_async_remote_copy(
                src_ref=part.at[pl.ds(8 * k, 8)], dst_ref=slots.at[near], send_sem=b_send.at[k], recv_sem=b_recv.at[near],
                device_id=line(owner), device_id_type=MESH).start()

        pl.when(near != owner)(send)
    for k in range(5):
        owner = 3 * k

        @pl.when(near == owner)
        def _(k=k, owner=owner):
            whole = part[8 * k:8 * k + 8, :]
            for m in range(16):
                if m != owner:
                    pltpu.make_async_remote_copy(
                        src_ref=part.at[pl.ds(8 * k, 8)], dst_ref=slots.at[m], send_sem=b_send.at[k],
                        recv_sem=b_recv.at[m], device_id=line(m), device_id_type=MESH).wait_recv()
                    whole = whole + slots[m]
            done[8 * k:8 * k + 8, :] = whole * scale
            for m in range(16):
                if m != owner:
                    pltpu.make_async_remote_copy(
                        src_ref=done.at[pl.ds(8 * k, 8)], dst_ref=done.at[pl.ds(8 * k, 8)], send_sem=c_send.at[m],
                        recv_sem=c_recv.at[k], device_id=line(m), device_id_type=MESH).start()
    for k in range(5):
        owner = 3 * k

        @pl.when(near != owner)
        def _(k=k, owner=owner):
            pltpu.make_async_remote_copy(
                src_ref=done.at[pl.ds(8 * k, 8)], dst_ref=done.at[pl.ds(8 * k, 8)], send_sem=c_send.at[0],
                recv_sem=c_recv.at[k], device_id=line(owner), device_id_type=MESH).wait_recv()

    lasts = []
    for d in range(1, 16):
        peer = (mine + d) % 16
        copy = pltpu.make_async_remote_copy(
            src_ref=done, dst_ref=o_ref.at[rows_of(mine)], send_sem=d_send.at[d], recv_sem=d_recv.at[d],
            device_id=plane(peer), device_id_type=MESH)
        copy.start()
        lasts.append(copy)
    o_ref[rows_of(mine), :] = done[...]

    for copy in firsts:
        copy.wait_send()
    for k in range(5):
        owner = 3 * k

        @pl.when(near != owner)
        def _(k=k, owner=owner):
            pltpu.make_async_remote_copy(
                src_ref=part.at[pl.ds(8 * k, 8)], dst_ref=slots.at[near], send_sem=b_send.at[k], recv_sem=b_recv.at[near],
                device_id=line(owner), device_id_type=MESH).wait_send()

        @pl.when(near == owner)
        def _(k=k, owner=owner):
            for m in range(16):
                if m != owner:
                    pltpu.make_async_remote_copy(
                        src_ref=done.at[pl.ds(8 * k, 8)], dst_ref=done.at[pl.ds(8 * k, 8)], send_sem=c_send.at[m],
                        recv_sem=c_recv.at[k], device_id=line(m), device_id_type=MESH).wait_send()
    for copy in lasts:
        copy.wait()


def summed(scale, values):
    dma = pltpu.SemaphoreType.DMA
    return pl.pallas_call(
        functools.partial(sum_kernel, scale),
        out_shape=jax.ShapeDtypeStruct((ROWS, 128), jnp.float32),
        in_specs=[pl.BlockSpec(memory_space=pltpu.VMEM)],
        out_specs=pl.BlockSpec(memory_space=pltpu.VMEM),
        scratch_shapes=[
            pltpu.VMEM((16, PART, 128), jnp.float32),
            pltpu.VMEM((PART, 128), jnp.float32),
            pltpu.VMEM((16, 8, 128), jnp.float32),
            pltpu.VMEM((PART, 128), jnp.float32),
            dma((16,)), dma((16,)), dma((8,)), dma((16,)), dma((16,)), dma((8,)), dma((16,)), dma((16,)),
        ],
        compiler_params=pltpu.CompilerParams(collective_id=1, has_side_effects=True),
        name="sums",
    )(values)


def per_device(coarse_field, cotangent, tconv_weight, conv_weight):
    batch, channels, rows_here, cols_here = cotangent.shape
    in_channels = coarse_field.shape[1]
    coarse = coarse_field.transpose(0, 2, 3, 1).reshape(-1, in_channels)
    coarse_grad, sums = section(
        coarse, cotangent.reshape(channels * rows_here, cols_here), tconv_weight.reshape(4 * channels, in_channels),
        conv_weight)
    total_cells = batch * rows_here * cols_here * lax.axis_size("lat") * lax.axis_size("lon")
    sums = summed(1.0 / math.sqrt(total_cells), sums)
    tiles = [sums[64 * m : 64 * m + 64] for m in range(4)] + [sums[256:320, :64]]
    coarse_grad = coarse_grad.reshape(batch, rows_here // 2, cols_here // 2, in_channels).transpose(0, 3, 1, 2)
    return coarse_grad, sums[320:576].reshape(4, channels, in_channels), jnp.concatenate(tiles, axis=1)


def solution(mesh):
    return jax.shard_map(
        per_device,
        mesh=mesh,
        in_specs=(P(None, None, "lat", "lon"), P(None, None, "lat", "lon"), P(), P()),
        out_specs=(P(None, None, "lat", "lon"), P(), P()),
        check_vma=False,
    )
```

profile of v0, /device:TPU:1, one launch (start us, length us, event | category | flops | bytes accessed | tf_op | source)
XLA Modules:
  0.0 59.1 jit_solution(5614013225573849510)
XLA Ops:
  0.6 0.0 copy-start
  0.6 1.2 %copy-done = bf16[1,64,64,128]{3,2,1,0:T(8,128)(2,1)S(1)} copy-done((bf16[1,64,64,128]{3,2,1,0:T(8,128)(2,1)S(1)}, bf16[1,64,64,128]{3,2,1,0:T(8,128)(2,1)}, u32[]{:S(2)}) %copy-start) | copy-done | bytes 1048600
  1.9 0.0 copy-start.1
  1.9 1.0 %copy-done.1 = bf16[1,128,32,64]{1,3,2,0:T(8,128)(2,1)S(1)} copy-done((bf16[1,128,32,64]{1,3,2,0:T(8,128)(2,1)S(1)}, bf16[1,128,32,64]{1,3,2,0:T(8,128)(2,1)}, u32[]{:S(2)}) %copy-start.1) | copy-done | bytes 524312
  2.9 0.0 copy-start.3
  2.9 0.9 %copy-done.3 = bf16[64,576]{1,0:T(8,128)(2,1)S(1)} copy-done((bf16[64,576]{1,0:T(8,128)(2,1)S(1)}, bf16[64,576]{1,0:T(8,128)(2,1)}, u32[]{:S(2)}) %copy-start.3) | copy-done | bytes 73752
  3.8 0.0 copy-start.4
  3.8 0.8 %copy-done.4 = bf16[4,64,128]{2,1,0:T(8,128)(2,1)S(1)} copy-done((bf16[4,64,128]{2,1,0:T(8,128)(2,1)S(1)}, bf16[4,64,128]{2,1,0:T(8,128)(2,1)}, u32[]{:S(2)}) %copy-start.4) | copy-done | bytes 65560
  4.6 18.4 %section.1 = (bf16[2048,128]{1,0:T(8,128)(2,1)S(1)}, f32[640,128]{1,0:T(8,128)S(1)}) custom-call(bf16[2048,128]{1,0:T(8,128)(2,1)S(1)} %bitcast.10, bf16[4096,128]{1,0:T(8,128)(2,1)S(1)} %bitcast.9, bf16[256,128]{1,0:T(8,128)(2,1)S(1)} %bitcast.12, bf16[64,576]{1,0:T(8,128)(2,1)S(1)} %copy-done.3), custom_call_target="tpu_custom_call" | custom-call | tf_op jit(solution)/shard_map/section/pallas_call | solution.py:246
  23.0 0.0 copy-start.2
  23.0 0.7 %copy-done.2 = f32[640,128]{1,0:T(8,128)} copy-done((f32[640,128]{1,0:T(8,128)}, f32[640,128]{1,0:T(8,128)S(1)}, u32[]{:S(2)}) %copy-start.2) | copy-done | bytes 327704
  23.8 29.1 %sums.1 = f32[640,128]{1,0:T(8,128)} custom-call(f32[640,128]{1,0:T(8,128)} %copy-done.2), custom_call_target="tpu_custom_call" | custom-call | tf_op jit(solution)/shard_map/sums/pallas_call | solution.py:380
  52.9 0.8 %slice_dynamic-update-slice_fusion.4 = f32[64,576]{1,0:T(8,128)S(1)} fusion(f32[640,128]{1,0:T(8,128)} %sums.1), kind=kLoop, calls=%fused_computation.4 | loop fusion | bytes 65536
  53.7 0.8 %slice_dynamic-update-slice_fusion.3 = f32[64,576]{1,0:T(8,128)S(1)} fusion(f32[64,576]{1,0:T(8,128)S(1)} %slice_dynamic-update-slice_fusion.4, f32[640,128]{1,0:T(8,128)} %sums.1), kind=kLoop, calls=%fused_computation.3 | loop fusion | bytes 65536
  54.4 0.8 %slice_dynamic-update-slice_fusion.2 = f32[64,576]{1,0:T(8,128)S(1)} fusion(f32[64,576]{1,0:T(8,128)S(1)} %slice_dynamic-update-slice_fusion.3, f32[640,128]{1,0:T(8,128)} %sums.1), kind=kLoop, calls=%fused_computation.2 | loop fusion | bytes 65536
  55.2 0.8 %slice_dynamic-update-slice_fusion.1 = f32[64,576]{1,0:T(8,128)S(1)} fusion(f32[64,576]{1,0:T(8,128)S(1)} %slice_dynamic-update-slice_fusion.2, f32[640,128]{1,0:T(8,128)} %sums.1), kind=kLoop, calls=%fused_computation.1 | loop fusion | bytes 65536
  55.9 0.8 %slice_dynamic-update-slice_fusion = f32[64,576]{1,0:T(8,128)S(1)} fusion(f32[64,576]{1,0:T(8,128)S(1)} %slice_dynamic-update-slice_fusion.1, f32[640,128]{1,0:T(8,128)} %sums.1), kind=kLoop, calls=%fused_computation | loop fusion | bytes 49152 | tf_op jit(solution)/shard_map/concatenate | solution.py:408
  56.7 0.0 copy-start.5
  56.7 1.6 %slice.18 = f32[256,128]{1,0:T(8,128)} slice(f32[640,128]{1,0:T(8,128)} %sums.1), slice={[320:576], [0:128]} | slice | bytes 262144 | tf_op jit(solution)/shard_map/slice | solution.py:408
  58.3 0.8 %copy.12 = bf16[1,128,32,64]{1,3,2,0:T(8,128)(2,1)} copy(bf16[1,128,32,64]{1,3,2,0:T(8,128)(2,1)S(1)} %bitcast.11) | data formatting | bytes 1048576
  59.1 0.0 copy-done.5
Async XLA Ops:
  0.6 1.2 %copy-start = (bf16[1,64,64,128]{3,2,1,0:T(8,128)(2,1)S(1)}, bf16[1,64,64,128]{3,2,1,0:T(8,128)(2,1)}, u32[]{:S(2)}) copy-start(bf16[1,64,64,128]{3,2,1,0:T(8,128)(2,1)} %param.5) | copy-start | bytes 3145732
  1.9 1.0 %copy-start.1 = (bf16[1,128,32,64]{1,3,2,0:T(8,128)(2,1)S(1)}, bf16[1,128,32,64]{1,3,2,0:T(8,128)(2,1)}, u32[]{:S(2)}) copy-start(bf16[1,128,32,64]{1,3,2,0:T(8,128)(2,1)} %param.4) | copy-start | bytes 1572868
  2.9 0.9 %copy-start.3 = (bf16[64,576]{1,0:T(8,128)(2,1)S(1)}, bf16[64,576]{1,0:T(8,128)(2,1)}, u32[]{:S(2)}) copy-start(bf16[64,576]{1,0:T(8,128)(2,1)} %conv_ref.1) | copy-start | bytes 221188
  3.8 0.8 %copy-start.4 = (bf16[4,64,128]{2,1,0:T(8,128)(2,1)S(1)}, bf16[4,64,128]{2,1,0:T(8,128)(2,1)}, u32[]{:S(2)}) copy-start(bf16[4,64,128]{2,1,0:T(8,128)(2,1)} %param.6) | copy-start | bytes 196612
  23.0 0.7 %copy-start.2 = (f32[640,128]{1,0:T(8,128)}, f32[640,128]{1,0:T(8,128)S(1)}, u32[]{:S(2)}) copy-start(f32[640,128]{1,0:T(8,128)S(1)} %get-tuple-element.6.x_ref) | copy-start | bytes 983044
  56.7 2.4 %copy-start.5 = (f32[64,576]{1,0:T(8,128)}, f32[64,576]{1,0:T(8,128)S(1)}, u32[]{:S(2)}) copy-start(f32[64,576]{1,0:T(8,128)S(1)} %slice_dynamic-update-slice_fusion) | copy-start | bytes 442372
where the time goes:
time: 59.8 us; the launch traced here: 59.1 us
  Pallas kernels  47.5 us (79%)
  local copies, waits for them, and re-layouts  10.9 us (18%)
  between operations  0.67 us (1%)
    pallas_call x1, Pallas kernels, summed(): pl.pallas_call(functools.partial(sum_kernel, scale), out_shape=jax.ShapeD...  29.1 us
    pallas_call x1, Pallas kernels, section(): pl.pallas_call(section_kernel, out_shape=(jax.ShapeDtypeStruct((cells, 12...  18.4 us
    unnamed x17, local copies, waits for them, and re-layouts  8.54 us
    slice x1, local copies, waits for them, and re-layouts, per_device(): sums[320:576].reshape(4, channels, in_channels)  1.63 us

commit v1 on v0

--- a/solution.py
+++ b/solution.py
@@ -11,6 +11,7 @@
 MESH = pl.DeviceIdType.MESH
 F32, BF16 = jnp.float32, jnp.bfloat16
 OWN, BESIDE = 0, 1
+VMEM_LIMIT = 62 * 2**20
 
 
 def row_step(source, half, p):
@@ -51,13 +52,112 @@
     return jnp.dot(a, b, preferred_element_type=F32)
 
 
+class Sum:
+    def __init__(self, source, half, arrived, seen, along, final, scale, send, recv):
+        self.source, self.half, self.arrived, self.seen, self.along, self.final = source, half, arrived, seen, along, final
+        self.scale, self.send, self.recv = scale, send, recv
+        self.lat, lon = lax.axis_index("lat"), lax.axis_index("lon")
+        self.lats, lons = lax.axis_size("lat"), lax.axis_size("lon")
+        self.side = lons // 2
+        self.members, self.length = 2 * self.lats, lons // 4
+        self.far = jnp.where(lon >= self.side, 1, 0)
+        self.near = lon - self.far * self.side
+        self.z, self.core = self.near // 2, self.near % 2
+        self.mine = self.far * self.lats + self.lat
+
+    def other(self):
+        return {"lat": self.lat, "lon": self.far * self.side + self.z * 2 + 1 - self.core}
+
+    def member(self, d):
+        flip, by = d // self.lats, d % self.lats
+        lat = self.lat + by
+        lat = jnp.where(lat >= self.lats, lat - self.lats, lat)
+        return lat, (1 - self.far if flip else self.far)
+
+    def plane(self, d):
+        lat, far = self.member(d)
+        return {"lat": lat, "lon": far * self.side + self.near}
+
+    def line(self, e):
+        z = self.z + e
+        z = jnp.where(z >= self.length, z - self.length, z)
+        return {"lat": self.lat, "lon": self.far * self.side + z * 2 + self.core}
+
+    def copy(self, source, target, phase, where):
+        return pltpu.make_async_remote_copy(
+            src_ref=source, dst_ref=target, send_sem=self.send.at[phase], recv_sem=self.recv.at[phase], device_id=where,
+            device_id_type=MESH)
+
+    def greet(self, barrier):
+        peers = [self.other()] + [self.plane(d) for d in range(1, self.members)]
+        peers += [self.line(e) for e in range(1, self.length)]
+        for peer in peers:
+            pl.semaphore_signal(barrier, inc=1, device_id=peer, device_id_type=MESH)
+        return len(peers)
+
+    def all_of(self, phase):
+        part = (self.arrived, self.seen.at[pl.ds(1, self.members - 1)], self.along.at[pl.ds(1, self.length - 1)],
+                self.seen.at[pl.ds(1, self.members - 1)], self.arrived)[phase]
+        return self.copy(part, part, phase, self.other())
+
+    def start(self):
+        self.copy(self.source.at[1 - self.core], self.arrived, 0, self.other()).start()
+
+    def scatter(self):
+        self.all_of(0).wait_recv()
+        self.half[...] = self.source[self.core] + self.arrived[...]
+        for d in range(1, self.members):
+            lat, far = self.member(d)
+            self.copy(self.half.at[far * self.lats + lat], self.seen.at[d], 1, self.plane(d)).start()
+
+    def pass_on(self):
+        self.all_of(1).wait_recv()
+        total = self.half[self.mine]
+        for d in range(1, self.members):
+            total = total + self.seen[d]
+        self.along[self.z] = total
+        for e in range(1, self.length):
+            self.copy(self.along.at[self.z], self.along.at[self.z], 2, self.line(e)).start()
+
+    def give_back(self):
+        self.all_of(2).wait_recv()
+        total = self.along[0]
+        for z in range(1, self.length):
+            total = total + self.along[z]
+        self.final[self.core, self.mine] = total * self.scale
+        for d in range(1, self.members):
+            at = self.final.at[self.core, self.mine]
+            self.copy(at, at, 3, self.plane(d)).start()
+
+    def bring_home(self):
+        self.all_of(3).wait_recv()
+        self.copy(self.final.at[self.core], self.final.at[self.core], 4, self.other()).start()
+
+    def end(self):
+        self.all_of(4).wait_recv()
+        for phase in range(5):
+            self.all_of(phase).wait_send()
+
+
 def section_kernel(
-    coarse_ref, cot_ref, tconv_ref, conv_ref, out_ref, sums_ref,
-    spread, tiles, west_out, east_out, west_in, east_in, patches, act_t, slope, pre_t, weights, pole_weights,
-    pole_patches, pole_extra, pole_sums, send_sem, recv_sem,
+    scale, coarse_hbm, cot_hbm, tconv_hbm, conv_hbm, out_ref, taps_out, conv_out,
+    coarse_ref, cot_ref, tconv_ref, conv_ref,
+    spread, tiles, west_out, east_out, west_in, east_in, patches, act_t, slope, pre, pre_t, weights, pole_weights,
+    pole_patches, pole_extra, pole_sums, send_sem, recv_sem, load_sem,
+    shares, half, arrived, seen, along, final, sum_send, sum_recv,
 ):
     pairs = coarse_ref.shape[0] // 64
     chunks = pairs // 4
+    loads = []
+    quarter = cot_ref.shape[0] // 4
+    for n in range(4):
+        at = pl.ds(n * quarter, quarter)
+        loads.append(pltpu.make_async_copy(cot_hbm.at[at], cot_ref.at[at], load_sem.at[n]))
+    for n, (source, target) in enumerate(((coarse_hbm, coarse_ref), (tconv_hbm, tconv_ref), (conv_hbm, conv_ref))):
+        loads.append(pltpu.make_async_copy(source, target, load_sem.at[4 + n]))
+    for load in loads:
+        load.start()
+
     lat, lon = lax.axis_index("lat"), lax.axis_index("lon")
     lats, lons = lax.axis_size("lat"), lax.axis_size("lon")
     at_north, at_south = lat == 0, lat == lats - 1
@@ -68,7 +168,10 @@
     def beside(which_lat, which_lon, by):
         return {"lat": which_lat, "lon": lax.rem(which_lon + by + lons, lons)}
 
+    total = Sum(shares, half, arrived, seen, along, final, scale, sum_send, sum_recv)
+
     barrier = pltpu.get_barrier_semaphore()
+    greeted = 8 + total.greet(barrier)
     for which in ((lat, lon, -1), (lat, lon, 1), (up_lat, up_lon, -1), (up_lat, up_lon, 0), (up_lat, up_lon, 1),
                   (down_lat, down_lon, -1), (down_lat, down_lon, 0), (down_lat, down_lon, 1)):
         pl.semaphore_signal(barrier, inc=1, device_id=beside(*which), device_id_type=MESH)
@@ -82,7 +185,9 @@
         spread[at, :] = times(cot_ref[at, :], order)
         return carry
 
-    lax.fori_loop(0, 64 * height // 512, reorder, 0)
+    for n in range(4):
+        loads[n].wait()
+        lax.fori_loop(n * (quarter // 512), (n + 1) * (quarter // 512), reorder, 0)
 
     def make_tile(i, carry):
         pair = jnp.concatenate(
@@ -96,7 +201,7 @@
 
     lax.fori_loop(0, pairs, make_tile, 0, unroll=2)
 
-    pl.semaphore_wait(barrier, 8)
+    pl.semaphore_wait(barrier, greeted)
     copies = []
 
     def send(source, target, sem, which, landed):
@@ -121,6 +226,9 @@
     send(west_out.at[tail], east_in.at[down_corner], 6, (down_lat, down_lon, -1), 2 + down_sem)
     send(east_out.at[tail], west_in.at[down_corner], 7, (down_lat, down_lon, 1), 4 + down_sem)
 
+    for load in loads[4:]:
+        load.wait()
+
     def activate(n, carry):
         at = pl.ds(pl.multiple_of(n * 256, 256), 256)
         up = across(coarse_ref[at, :], tconv_ref[...])
@@ -204,6 +312,23 @@
 
     lax.fori_loop(0, pairs, lay, 0, unroll=2)
 
+    for n in range(chunks):
+        at = slice(n * 256, n * 256 + 256)
+        grad = times(patches[at, :], weights[...])
+        if n == 0:
+            grad = jnp.concatenate([grad[:128] + pole_extra[0], grad[128:]], axis=0)
+        if n == chunks - 1:
+            grad = jnp.concatenate([grad[:128], grad[128:] + pole_extra[1]], axis=0)
+        rounded = (grad * slope[at, :]).astype(BF16)
+        pre[at, :] = rounded
+        pre_t[:, at] = rounded.T
+    members = shares.shape[1]
+    share = 256 // members
+    spare = 16 // members
+    taps_grad = times(pre_t[...], coarse_ref[...])
+    for m in range(members):
+        shares[1, m, :share] = taps_grad[share * m : share * m + share]
+
     found = {}
 
     def add(tap, value):
@@ -218,37 +343,57 @@
     for w, h, p, q, t in pole_blocks():
         at, col = 128 * p + 64 * q, w * 128 + h * 64
         add(t, pole_sums[at : at + 64, col : col + 64])
-    for m in range(5):
-        both = jnp.concatenate([found[2 * m], found[2 * m + 1] if m < 4 else jnp.zeros((64, 64), F32)], axis=0)
-        sums_ref[64 * m : 64 * m + 64, :] = both.T
+    for b in range(4):
+        both = jnp.concatenate([found[2 * b], found[2 * b + 1]], axis=0).T
+        for m in range(members):
+            low, high = max(64 * b, share * m), min(64 * b + 64, share * m + share)
+            if low < high:
+                shares[0, m, low - share * m : high - share * m] = both[low - 64 * b : high - 64 * b]
+    last_tap = found[8].T
+    last_tap = jnp.concatenate([last_tap[:32], last_tap[32:]], axis=1)
+    for m in range(members):
+        for core in range(2):
+            at = 16 * core + spare * m
+            shares[core, m, share:] = last_tap[at : at + spare]
+    total.start()
 
     for n in range(chunks):
         at = slice(n * 256, n * 256 + 256)
-        grad = times(patches[at, :], weights[...])
-        if n == 0:
-            grad = jnp.concatenate([grad[:128] + pole_extra[0], grad[128:]], axis=0)
-        if n == chunks - 1:
-            grad = jnp.concatenate([grad[:128], grad[128:] + pole_extra[1]], axis=0)
-        pre = (grad * slope[at, :]).astype(BF16)
-        pre_t[:, at] = pre.T
-        out_ref[at, :] = times(pre, tconv_ref[...]).astype(BF16)
-    sums_ref[320:576, :] = times(pre_t[...], coarse_ref[...])
-    sums_ref[576:, :] = jnp.zeros((64, 128), F32)
-
+        out_ref[at, :] = times(pre[at, :], tconv_ref[...]).astype(BF16)
+    total.scatter()
+    total.pass_on()
+    total.give_back()
+    total.bring_home()
     for copy in copies:
         copy.wait_send()
-
-
-def section(coarse, cotangent, tconv, conv):
+    total.end()
+    for m in range(members):
+        taps_out[share * m : share * m + share, :] = final[1, m, :share]
+        for low in range(share * m, share * m + share, min(share, 64)):
+            high, b = low + min(share, 64), low // 64
+            conv_out[low - 64 * b : high - 64 * b, 128 * b : 128 * b + 128] = final[0, m, low - share * m : high - share * m]
+        for core in range(2):
+            at = 16 * core + spare * m
+            line = final[core, m, share:]
+            conv_out[at : at + spare, 512:] = line[:, :64]
+            conv_out[32 + at : 32 + at + spare, 512:] = line[:, 64:]
+
+
+def section(scale, coarse, cotangent, tconv, conv):
     cells = coarse.shape[0]
     pairs = cells // 64
-    vmem = pl.BlockSpec(memory_space=pltpu.VMEM)
+    members, length = 2 * lax.axis_size("lat"), lax.axis_size("lon") // 4
+    chunk = 272 // members
+    vmem, hbm = pl.BlockSpec(memory_space=pltpu.VMEM), pl.BlockSpec(memory_space=pltpu.HBM)
     return pl.pallas_call(
-        section_kernel,
-        out_shape=(jax.ShapeDtypeStruct((cells, 128), BF16), jax.ShapeDtypeStruct((ROWS, 128), F32)),
-        in_specs=[vmem] * 4,
-        out_specs=(vmem, vmem),
+        functools.partial(section_kernel, scale),
+        out_shape=(jax.ShapeDtypeStruct((cells, 128), BF16), jax.ShapeDtypeStruct((256, 128), F32),
+                   jax.ShapeDtypeStruct(conv.shape, F32)),
+        in_specs=[hbm] * 4,
+        out_specs=(vmem, vmem, vmem),
         scratch_shapes=[
+            pltpu.VMEM(coarse.shape, BF16), pltpu.VMEM(cotangent.shape, BF16), pltpu.VMEM(tconv.shape, BF16),
+            pltpu.VMEM(conv.shape, BF16),
             pltpu.VMEM((cells * 2, 128), F32),
             pltpu.VMEM((pairs + 2, 4, 64, 128), BF16),
             pltpu.VMEM((pairs, 128), F32), pltpu.VMEM((pairs, 128), F32),
@@ -256,156 +401,35 @@
             pltpu.VMEM((cells, 1024), BF16),
             pltpu.VMEM((256, cells), BF16),
             pltpu.VMEM((cells, 256), F32),
+            pltpu.VMEM((cells, 256), BF16),
             pltpu.VMEM((256, cells), BF16),
             pltpu.VMEM((1024, 256), BF16),
             pltpu.VMEM((512, 256), BF16),
             pltpu.VMEM((128, 512), BF16),
             pltpu.VMEM((2, 128, 256), F32),
             pltpu.VMEM((256, 512), F32),
-            pltpu.SemaphoreType.DMA((8,)), pltpu.SemaphoreType.DMA((8,)),
+            pltpu.SemaphoreType.DMA((8,)), pltpu.SemaphoreType.DMA((8,)), pltpu.SemaphoreType.DMA((7,)),
+            pltpu.VMEM((2, members, chunk, 128), F32),
+            pltpu.VMEM((members, chunk, 128), F32), pltpu.VMEM((members, chunk, 128), F32),
+            pltpu.VMEM((members, chunk, 128), F32), pltpu.VMEM((length, chunk, 128), F32),
+            pltpu.VMEM((2, members, chunk, 128), F32),
+            pltpu.SemaphoreType.DMA((5,)), pltpu.SemaphoreType.DMA((5,)),
         ],
-        compiler_params=pltpu.CompilerParams(collective_id=0, has_side_effects=True, vmem_limit_bytes=40 * 2**20),
+        compiler_params=pltpu.CompilerParams(collective_id=0, has_side_effects=True, vmem_limit_bytes=VMEM_LIMIT),
         name="section",
     )(coarse, cotangent, tconv, conv)
-
-
-ROWS = 640
-PART = 40
-
-
-def sum_kernel(scale, x_ref, o_ref, seen, part, slots, done, a_send, a_recv, b_send, b_recv, c_send, c_recv, d_send, d_recv):
-    lat, lon = lax.axis_index("lat"), lax.axis_index("lon")
-    far, near = lon // 16, lon % 16
-    mine = far * 8 + lat
-
-    def plane(member):
-        return {"lat": member % 8, "lon": (member // 8) * 16 + near}
-
-    def line(member):
-        return {"lat": lat, "lon": far * 16 + member}
-
-    barrier = pltpu.get_barrier_semaphore()
-    for d in range(1, 16):
-        pl.semaphore_signal(barrier, inc=1, device_id=plane((mine + d) % 16), device_id_type=MESH)
-        pl.semaphore_signal(barrier, inc=1, device_id=line((near + d) % 16), device_id_type=MESH)
-    pl.semaphore_wait(barrier, 30)
-
-    def rows_of(member):
-        return pl.ds(pl.multiple_of(member * PART, 8), PART)
-
-    firsts = []
-    for d in range(1, 16):
-        peer = (mine + d) % 16
-        copy = pltpu.make_async_remote_copy(
-            src_ref=x_ref.at[rows_of(peer)], dst_ref=seen.at[d], send_sem=a_send.at[d], recv_sem=a_recv.at[d],
-            device_id=plane(peer), device_id_type=MESH)
-        copy.start()
-        firsts.append(copy)
-    total = x_ref[rows_of(mine), :]
-    for d in range(1, 16):
-        firsts[d - 1].wait_recv()
-        total = total + seen[d]
-    part[...] = total
-
-    for k in range(5):
-        owner = 3 * k
-
-        def send(k=k, owner=owner):
-            pltpu.make_async_remote_copy(
-                src_ref=part.at[pl.ds(8 * k, 8)], dst_ref=slots.at[near], send_sem=b_send.at[k], recv_sem=b_recv.at[near],
-                device_id=line(owner), device_id_type=MESH).start()
-
-        pl.when(near != owner)(send)
-    for k in range(5):
-        owner = 3 * k
-
-        @pl.when(near == owner)
-        def _(k=k, owner=owner):
-            whole = part[8 * k:8 * k + 8, :]
-            for m in range(16):
-                if m != owner:
-                    pltpu.make_async_remote_copy(
-                        src_ref=part.at[pl.ds(8 * k, 8)], dst_ref=slots.at[m], send_sem=b_send.at[k],
-                        recv_sem=b_recv.at[m], device_id=line(m), device_id_type=MESH).wait_recv()
-                    whole = whole + slots[m]
-            done[8 * k:8 * k + 8, :] = whole * scale
-            for m in range(16):
-                if m != owner:
-                    pltpu.make_async_remote_copy(
-                        src_ref=done.at[pl.ds(8 * k, 8)], dst_ref=done.at[pl.ds(8 * k, 8)], send_sem=c_send.at[m],
-                        recv_sem=c_recv.at[k], device_id=line(m), device_id_type=MESH).start()
-    for k in range(5):
-        owner = 3 * k
-
-        @pl.when(near != owner)
-        def _(k=k, owner=owner):
-            pltpu.make_async_remote_copy(
-                src_ref=done.at[pl.ds(8 * k, 8)], dst_ref=done.at[pl.ds(8 * k, 8)], send_sem=c_send.at[0],
-                recv_sem=c_recv.at[k], device_id=line(owner), device_id_type=MESH).wait_recv()
-
-    lasts = []
-    for d in range(1, 16):
-        peer = (mine + d) % 16
-        copy = pltpu.make_async_remote_copy(
-            src_ref=done, dst_ref=o_ref.at[rows_of(mine)], send_sem=d_send.at[d], recv_sem=d_recv.at[d],
-            device_id=plane(peer), device_id_type=MESH)
-        copy.start()
-        lasts.append(copy)
-    o_ref[rows_of(mine), :] = done[...]
-
-    for copy in firsts:
-        copy.wait_send()
-    for k in range(5):
-        owner = 3 * k
-
-        @pl.when(near != owner)
-        def _(k=k, owner=owner):
-            pltpu.make_async_remote_copy(
-                src_ref=part.at[pl.ds(8 * k, 8)], dst_ref=slots.at[near], send_sem=b_send.at[k], recv_sem=b_recv.at[near],
-                device_id=line(owner), device_id_type=MESH).wait_send()
-
-        @pl.when(near == owner)
-        def _(k=k, owner=owner):
-            for m in range(16):
-                if m != owner:
-                    pltpu.make_async_remote_copy(
-                        src_ref=done.at[pl.ds(8 * k, 8)], dst_ref=done.at[pl.ds(8 * k, 8)], send_sem=c_send.at[m],
-                        recv_sem=c_recv.at[k], device_id=line(m), device_id_type=MESH).wait_send()
-    for copy in lasts:
-        copy.wait()
-
-
-def summed(scale, values):
-    dma = pltpu.SemaphoreType.DMA
-    return pl.pallas_call(
-        functools.partial(sum_kernel, scale),
-        out_shape=jax.ShapeDtypeStruct((ROWS, 128), jnp.float32),
-        in_specs=[pl.BlockSpec(memory_space=pltpu.VMEM)],
-        out_specs=pl.BlockSpec(memory_space=pltpu.VMEM),
-        scratch_shapes=[
-            pltpu.VMEM((16, PART, 128), jnp.float32),
-            pltpu.VMEM((PART, 128), jnp.float32),
-            pltpu.VMEM((16, 8, 128), jnp.float32),
-            pltpu.VMEM((PART, 128), jnp.float32),
-            dma((16,)), dma((16,)), dma((8,)), dma((16,)), dma((16,)), dma((8,)), dma((16,)), dma((16,)),
-        ],
-        compiler_params=pltpu.CompilerParams(collective_id=1, has_side_effects=True),
-        name="sums",
-    )(values)
 
 
 def per_device(coarse_field, cotangent, tconv_weight, conv_weight):
     batch, channels, rows_here, cols_here = cotangent.shape
     in_channels = coarse_field.shape[1]
     coarse = coarse_field.transpose(0, 2, 3, 1).reshape(-1, in_channels)
-    coarse_grad, sums = section(
-        coarse, cotangent.reshape(channels * rows_here, cols_here), tconv_weight.reshape(4 * channels, in_channels),
-        conv_weight)
     total_cells = batch * rows_here * cols_here * lax.axis_size("lat") * lax.axis_size("lon")
-    sums = summed(1.0 / math.sqrt(total_cells), sums)
-    tiles = [sums[64 * m : 64 * m + 64] for m in range(4)] + [sums[256:320, :64]]
+    coarse_grad, tconv_grad, conv_grad = section(
+        1.0 / math.sqrt(total_cells), coarse, cotangent.reshape(channels * rows_here, cols_here),
+        tconv_weight.reshape(4 * channels, in_channels), conv_weight)
     coarse_grad = coarse_grad.reshape(batch, rows_here // 2, cols_here // 2, in_channels).transpose(0, 3, 1, 2)
-    return coarse_grad, sums[320:576].reshape(4, channels, in_channels), jnp.concatenate(tiles, axis=1)
+    return coarse_grad, tconv_grad.reshape(4, channels, in_channels), conv_grad
 
 
 def solution(mesh):

time: 59.8 us -> 43.5 us (0.73)
  Pallas kernels: 47.5 us -> 39.2 us
  local copies, waits for them, and re-layouts: 10.9 us -> 3.54 us
    pallas_call x2 -> x1, Pallas kernels: 47.5 us -> 39.2 us  [section(): pl.pallas_call(functools.partial(section_kernel, scale), out_shape=(jax.S...]
    unnamed x17 -> x7, local copies, waits for them, and re-layouts: 8.54 us -> 3.54 us
    slice x1 -> x0, local copies, waits for them, and re-layouts: 1.63 us -> none  [per_device(): sums[320:576].reshape(4, channels, in_channels)]
    concatenate x1 -> x0, local copies, waits for them, and re-layouts: 0.76 us -> none  [per_device(): jnp.concatenate(tiles, axis=1)]
where the time goes in v1:
time: 43.5 us; the launch traced here: 43.4 us
  Pallas kernels  39.2 us (90%)
  local copies, waits for them, and re-layouts  3.54 us (8%)
  between operations  0.65 us (1%)
    pallas_call x1, Pallas kernels, section(): pl.pallas_call(functools.partial(section_kernel, scale), out_shape=(jax.S...  39.2 us
    unnamed x7, local copies, waits for them, and re-layouts  3.54 us

profile of v1, /device:TPU:1, one launch (start us, length us, event | category | flops | bytes accessed | tf_op | source)
XLA Modules:
  0.0 43.4 jit_solution(2864237317704734857)
XLA Ops:
  0.6 39.2 %section.1 = (bf16[2048,128]{1,0:T(8,128)(2,1)}, f32[256,128]{1,0:T(8,128)}, f32[64,576]{1,0:T(8,128)}) custom-call(bf16[2048,128]{1,0:T(8,128)(2,1)} %bitcast.10, bf16[4096,128]{1,0:T(8,128)(2,1)} %bitcast.9, bf16[256,128]{1,0:T(8,128)(2,1)} %bitcast.13, bf16[64,576]{1,0:T(8,128)(2,1)} %conv_hbm.1), custom_call_target="tpu_custom_call" | custom-call | tf_op jit(solution)/shard_map/section/pallas_call | solution.py:388
  39.9 0.0 copy-start.1
  39.9 1.9 %copy.10 = bf16[1,128,32,64]{1,3,2,0:T(8,128)(2,1)} copy(bf16[1,128,32,64]{1,3,2,0:T(8,128)(2,1)} %bitcast.11) | data formatting | bytes 1048576
  41.8 0.0 copy-done.1
  41.8 0.0 copy-start
  41.8 0.7 %copy.11 = f32[4,64,128]{2,1,0:T(8,128)} copy(f32[4,64,128]{2,1,0:T(8,128)S(1)} %bitcast.12) | data formatting | bytes 262144
  42.4 0.3 copy-done
  42.7 0.7 %copy.12 = f32[64,576]{1,0:T(8,128)} copy(f32[64,576]{1,0:T(8,128)S(1)} %copy-done) | data formatting | bytes 294912
Async XLA Ops:
  39.9 1.9 %copy-start.1 = (f32[256,128]{1,0:T(8,128)S(1)}, f32[256,128]{1,0:T(8,128)}, u32[]{:S(2)}) copy-start(f32[256,128]{1,0:T(8,128)} %get-tuple-element.7) | copy-start | bytes 393220
  41.8 1.0 %copy-start = (f32[64,576]{1,0:T(8,128)S(1)}, f32[64,576]{1,0:T(8,128)}, u32[]{:S(2)}) copy-start(f32[64,576]{1,0:T(8,128)} %get-tuple-element.14) | copy-start | bytes 442372

commit v2 on v1

--- a/solution.py
+++ b/solution.py
@@ -11,7 +11,7 @@
 MESH = pl.DeviceIdType.MESH
 F32, BF16 = jnp.float32, jnp.bfloat16
 OWN, BESIDE = 0, 1
-VMEM_LIMIT = 62 * 2**20
+VMEM_LIMIT = 48 * 2**20
 
 
 def row_step(source, half, p):
@@ -50,6 +50,14 @@
 
 def times(a, b):
     return jnp.dot(a, b, preferred_element_type=F32)
+
+
+def each(low, high, act):
+    def step(n, carry):
+        act(n)
+        return carry
+
+    lax.fori_loop(low, high, step, 0)
 
 
 class Sum:
@@ -69,10 +77,9 @@
         return {"lat": self.lat, "lon": self.far * self.side + self.z * 2 + 1 - self.core}
 
     def member(self, d):
-        flip, by = d // self.lats, d % self.lats
-        lat = self.lat + by
-        lat = jnp.where(lat >= self.lats, lat - self.lats, lat)
-        return lat, (1 - self.far if flip else self.far)
+        flip = d >= self.lats
+        lat = self.lat + jnp.where(flip, d - self.lats, d)
+        return jnp.where(lat >= self.lats, lat - self.lats, lat), jnp.where(flip, 1 - self.far, self.far)
 
     def plane(self, d):
         lat, far = self.member(d)
@@ -89,11 +96,13 @@
             device_id_type=MESH)
 
     def greet(self, barrier):
-        peers = [self.other()] + [self.plane(d) for d in range(1, self.members)]
-        peers += [self.line(e) for e in range(1, self.length)]
-        for peer in peers:
+        def signal(peer):
             pl.semaphore_signal(barrier, inc=1, device_id=peer, device_id_type=MESH)
-        return len(peers)
+
+        signal(self.other())
+        each(1, self.members, lambda d: signal(self.plane(d)))
+        each(1, self.length, lambda e: signal(self.line(e)))
+        return self.members + self.length - 1
 
     def all_of(self, phase):
         part = (self.arrived, self.seen.at[pl.ds(1, self.members - 1)], self.along.at[pl.ds(1, self.length - 1)],
@@ -106,9 +115,12 @@
     def scatter(self):
         self.all_of(0).wait_recv()
         self.half[...] = self.source[self.core] + self.arrived[...]
-        for d in range(1, self.members):
+
+        def send(d):
             lat, far = self.member(d)
             self.copy(self.half.at[far * self.lats + lat], self.seen.at[d], 1, self.plane(d)).start()
+
+        each(1, self.members, send)
 
     def pass_on(self):
         self.all_of(1).wait_recv()
@@ -116,8 +128,7 @@
         for d in range(1, self.members):
             total = total + self.seen[d]
         self.along[self.z] = total
-        for e in range(1, self.length):
-            self.copy(self.along.at[self.z], self.along.at[self.z], 2, self.line(e)).start()
+        each(1, self.length, lambda e: self.copy(self.along.at[self.z], self.along.at[self.z], 2, self.line(e)).start())
 
     def give_back(self):
         self.all_of(2).wait_recv()
@@ -125,9 +136,8 @@
         for z in range(1, self.length):
             total = total + self.along[z]
         self.final[self.core, self.mine] = total * self.scale
-        for d in range(1, self.members):
-            at = self.final.at[self.core, self.mine]
-            self.copy(at, at, 3, self.plane(d)).start()
+        at = self.final.at[self.core, self.mine]
+        each(1, self.members, lambda d: self.copy(at, at, 3, self.plane(d)).start())
 
     def bring_home(self):
         self.all_of(3).wait_recv()
@@ -219,12 +229,34 @@
     up_sem, down_sem = jnp.where(at_north, 0, 1), jnp.where(at_south, 1, 0)
     send(west_out, east_in.at[pl.ds(8, pairs)], 0, (lat, lon, -1), 6)
     send(east_out, west_in.at[pl.ds(8, pairs)], 1, (lat, lon, 1), 7)
-    send(tiles.at[1, pl.ds(0, 2)], tiles.at[up_slot, pl.ds(0, 2)], 2, (up_lat, up_lon, 0), up_sem)
-    send(tiles.at[pairs, pl.ds(0, 2)], tiles.at[down_slot, pl.ds(0, 2)], 3, (down_lat, down_lon, 0), down_sem)
+    send(tiles.at[1], tiles.at[up_slot], 2, (up_lat, up_lon, 0), up_sem)
+    send(tiles.at[pairs], tiles.at[down_slot], 3, (down_lat, down_lon, 0), down_sem)
     send(west_out.at[head], east_in.at[up_corner], 4, (up_lat, up_lon, -1), 2 + up_sem)
     send(east_out.at[head], west_in.at[up_corner], 5, (up_lat, up_lon, 1), 4 + up_sem)
     send(west_out.at[tail], east_in.at[down_corner], 6, (down_lat, down_lon, -1), 2 + down_sem)
     send(east_out.at[tail], west_in.at[down_corner], 7, (down_lat, down_lon, 1), 4 + down_sem)
+
+    row = lax.broadcasted_iota(jnp.int32, (64, 128), 0)
+
+    def beside_tile(even, odd, west_row, east_row):
+        return (jnp.where(row == 0, west_row, pltpu.roll(odd, 1, 0)), jnp.where(row == 63, east_row, pltpu.roll(even, 63, 0)))
+
+    def place(i, w, low, high, value):
+        def at(block):
+            return pl.ds(pl.multiple_of(block * 64 + low, 16), high - low)
+
+        patches[at(i + 1), 256 * w : 256 * w + 128] = value
+        patches[at(i), 256 * w + 128 : 256 * w + 192] = value[:, :64]
+        patches[at(i + 2), 256 * w + 192 : 256 * w + 256] = value[:, 64:]
+
+    def lay(i, carry):
+        even, odd = tiles[i + 1, 0], tiles[i + 1, 1]
+        west, east = beside_tile(even.astype(F32), odd.astype(F32), 0.0, 0.0)
+        for w, value in enumerate((even, odd, west.astype(BF16), east.astype(BF16))):
+            place(i, w, 0, 64, value)
+        return carry
+
+    lax.fori_loop(0, pairs, lay, 0, unroll=2)
 
     for load in loads[4:]:
         load.wait()
@@ -258,63 +290,56 @@
     pole_sums[...] = jnp.zeros_like(pole_sums)
 
     for landed, source in enumerate(
-        (tiles.at[0, pl.ds(0, 2)], tiles.at[0, pl.ds(0, 2)], east_in.at[head], east_in.at[head], west_in.at[head],
+        (tiles.at[0], tiles.at[0], east_in.at[head], east_in.at[head], west_in.at[head],
          west_in.at[head], east_in.at[pl.ds(8, pairs)], west_in.at[pl.ds(8, pairs)])):
         pltpu.make_async_remote_copy(
             src_ref=source, dst_ref=source, send_sem=send_sem.at[0], recv_sem=recv_sem.at[landed],
             device_id=beside(lat, lon, 1), device_id_type=MESH).wait_recv()
 
-    line = lax.broadcasted_iota(jnp.int32, (64, 128), 0)
-
-    def shift(i, west_row, east_row):
-        even, odd = tiles[i, 0].astype(F32), tiles[i, 1].astype(F32)
-        tiles[i, 2] = jnp.where(line == 0, west_in[pl.ds(west_row, 1), :], pltpu.roll(odd, 1, 0)).astype(BF16)
-        tiles[i, 3] = jnp.where(line == 63, east_in[pl.ds(east_row, 1), :], pltpu.roll(even, 63, 0)).astype(BF16)
-
-    def shift_own(i, carry):
-        shift(i, i + 7, i + 7)
-        return carry
-
-    north_row, south_row = jnp.where(at_north, 0, 7), jnp.where(at_south, pairs + 15, pairs + 8)
-    shift(0, north_row, north_row)
-    shift(pairs + 1, south_row, south_row)
-    lax.fori_loop(1, pairs + 1, shift_own, 0, unroll=2)
+    edge = lax.broadcasted_iota(jnp.int32, (16, 128), 0)
+
+    def mend(i, carry):
+        for w, low, at_row, halo in ((2, 0, 0, west_in), (3, 48, 15, east_in)):
+            block = patches[pl.ds(pl.multiple_of((i + 1) * 64 + low, 16), 16), 256 * w : 256 * w + 128].astype(F32)
+            block = jnp.where(edge == at_row, halo[pl.ds(i + 8, 1), :], block).astype(BF16)
+            place(i, w, low, low + 16, block)
+        return carry
+
+    lax.fori_loop(0, pairs, mend, 0, unroll=2)
+
+    def halo_windows(slot, corner):
+        even, odd = tiles[slot, 0].astype(F32), tiles[slot, 1].astype(F32)
+        return (even, odd) + beside_tile(even, odd, west_in[pl.ds(corner, 1), :], east_in[pl.ds(corner, 1), :])
+
+    north = halo_windows(0, jnp.where(at_north, 0, 7))
+    south = halo_windows(pairs + 1, jnp.where(at_south, pairs + 15, pairs + 8))
+    last = pairs * 64
+    for w in range(4):
+        patches[64:128, 256 * w + 192 : 256 * w + 256] = jnp.where(at_north, 0.0, north[w][:, 64:]).astype(BF16)
+        patches[last : last + 64, 256 * w + 128 : 256 * w + 192] = jnp.where(at_south, 0.0, south[w][:, :64]).astype(BF16)
 
     lane = lax.broadcasted_iota(jnp.int32, (64, 128), 1)
     blank = jnp.zeros((64, 128), BF16)
 
-    def take_pole(slot, first, keep):
-        for w in range(4):
-            pole_patches[first : first + 64, 128 * w : 128 * w + 128] = jnp.where(keep, tiles[slot, w].astype(F32), 0.0).astype(BF16)
-            pole_patches[64 - first : 128 - first, 128 * w : 128 * w + 128] = blank
-            tiles[slot, w] = blank
-
-    last = pairs * 64
-
     @pl.when(at_north)
     def _():
-        take_pole(0, 0, lane < 64)
+        for w in range(4):
+            pole_patches[:64, 128 * w : 128 * w + 128] = jnp.where(lane < 64, north[w], 0.0).astype(BF16)
+            pole_patches[64:, 128 * w : 128 * w + 128] = blank
         pole_extra[0] = times(pole_patches[...], pole_weights[...])
         pole_sums[...] = times(act_t[:, :128], pole_patches[...])
 
     @pl.when(at_south)
     def _():
-        take_pole(pairs + 1, 64, lane >= 64)
+        for w in range(4):
+            pole_patches[:64, 128 * w : 128 * w + 128] = blank
+            pole_patches[64:, 128 * w : 128 * w + 128] = jnp.where(lane < 64, 0.0, south[w]).astype(BF16)
         pole_extra[1] = times(pole_patches[...], pole_weights[...])
         pole_sums[...] = times(act_t[:, last - 128 :], pole_patches[...])
 
-    def lay(i, carry):
-        at = pl.ds(pl.multiple_of(i * 64, 64), 64)
-        for w in range(4):
-            patches[at, 256 * w : 256 * w + 128] = tiles[i + 1, w]
-            patches[at, 256 * w + 128 : 256 * w + 256] = jnp.where(lane < 64, tiles[i + 2, w], tiles[i, w])
-        return carry
-
-    lax.fori_loop(0, pairs, lay, 0, unroll=2)
-
     for n in range(chunks):
         at = slice(n * 256, n * 256 + 256)
-        grad = times(patches[at, :], weights[...])
+        grad = times(patches[n * 256 + 64 : n * 256 + 320, :], weights[...])
         if n == 0:
             grad = jnp.concatenate([grad[:128] + pole_extra[0], grad[128:]], axis=0)
         if n == chunks - 1:
@@ -335,7 +360,7 @@
         found[tap] = value if tap not in found else found[tap] + value
 
     for w in range(4):
-        grads = times(act_t[...], patches[:, 256 * w : 256 * w + 256])
+        grads = times(act_t[...], patches[64 : last + 64, 256 * w : 256 * w + 256])
         for s, ww, h, p, q, t in window_blocks():
             if ww == w:
                 at, col = 128 * p + 64 * q, s * 128 + h * 64
@@ -387,18 +412,17 @@
     vmem, hbm = pl.BlockSpec(memory_space=pltpu.VMEM), pl.BlockSpec(memory_space=pltpu.HBM)
     return pl.pallas_call(
         functools.partial(section_kernel, scale),
-        out_shape=(jax.ShapeDtypeStruct((cells, 128), BF16), jax.ShapeDtypeStruct((256, 128), F32),
-                   jax.ShapeDtypeStruct(conv.shape, F32)),
+        out_shape=(pltpu.VMEM((cells, 128), BF16), pltpu.VMEM((256, 128), F32), pltpu.VMEM(conv.shape, F32)),
         in_specs=[hbm] * 4,
         out_specs=(vmem, vmem, vmem),
         scratch_shapes=[
             pltpu.VMEM(coarse.shape, BF16), pltpu.VMEM(cotangent.shape, BF16), pltpu.VMEM(tconv.shape, BF16),
             pltpu.VMEM(conv.shape, BF16),
             pltpu.VMEM((cells * 2, 128), F32),
-            pltpu.VMEM((pairs + 2, 4, 64, 128), BF16),
+            pltpu.VMEM((pairs + 2, 2, 64, 128), BF16),
             pltpu.VMEM((pairs, 128), F32), pltpu.VMEM((pairs, 128), F32),
             pltpu.VMEM((pairs + 16, 128), F32), pltpu.VMEM((pairs + 16, 128), F32),
-            pltpu.VMEM((cells, 1024), BF16),
+            pltpu.VMEM((cells + 128, 1024), BF16),
             pltpu.VMEM((256, cells), BF16),
             pltpu.VMEM((cells, 256), F32),
             pltpu.VMEM((cells, 256), BF16),
@@ -417,7 +441,7 @@
         ],
         compiler_params=pltpu.CompilerParams(collective_id=0, has_side_effects=True, vmem_limit_bytes=VMEM_LIMIT),
         name="section",
-    )(coarse, cotangent, tconv, conv)
+    )(*(pltpu.with_memory_space_constraint(x, pltpu.HBM) for x in (coarse, cotangent, tconv, conv)))
 
 
 def per_device(coarse_field, cotangent, tconv_weight, conv_weight):

time: 43.5 us -> 40.6 us (0.933)
  Pallas kernels: 39.2 us -> 37.7 us
  local copies, waits for them, and re-layouts: 3.54 us -> 2.12 us
    pallas_call x1, Pallas kernels: 39.2 us -> 37.7 us  [section(): pl.pallas_call(functools.partial(section_kernel, scale), out_shape=(pltpu...]
    unnamed x7 -> x3, local copies, waits for them, and re-layouts: 3.54 us -> 2.12 us
where the time goes in v2:
time: 40.6 us; the launch traced here: 40.5 us
  Pallas kernels  37.7 us (93%)
  local copies, waits for them, and re-layouts  2.12 us (5%)
  between operations  0.64 us (2%)
    pallas_call x1, Pallas kernels, section(): pl.pallas_call(functools.partial(section_kernel, scale), out_shape=(pltpu...  37.7 us
    unnamed x3, local copies, waits for them, and re-layouts  2.12 us

profile of v2, /device:TPU:1, one launch (start us, length us, event | category | flops | bytes accessed | tf_op | source)
XLA Modules:
  0.0 40.5 jit_solution(15567798683911011945)
XLA Ops:
  0.6 37.7 %section.1 = (bf16[2048,128]{1,0:T(8,128)(2,1)S(1)}, f32[256,128]{1,0:T(8,128)S(1)}, f32[64,576]{1,0:T(8,128)S(1)}) custom-call(bf16[2048,128]{1,0:T(8,128)(2,1)} %bitcast.12, bf16[4096,128]{1,0:T(8,128)(2,1)} %bitcast.11, bf16[256,128]{1,0:T(8,128)(2,1)} %bitcast.13, bf16[64,576]{1,0:T(8,128)(2,1)} %conv_hbm.1), custom_call_target="tpu_custom_call" | custom-call | tf_op jit(solution)/shard_map/section/pallas_call | solution.py:413
  38.4 0.8 %copy.10 = bf16[1,128,32,64]{1,3,2,0:T(8,128)(2,1)} copy(bf16[1,128,32,64]{1,3,2,0:T(8,128)(2,1)S(1)} %bitcast.9) | data formatting | bytes 1048576
  39.2 0.7 %copy.11 = f32[4,64,128]{2,1,0:T(8,128)} copy(f32[4,64,128]{2,1,0:T(8,128)S(1)} %bitcast.10) | data formatting | bytes 262144
  39.8 0.7 %copy.12 = f32[64,576]{1,0:T(8,128)} copy(f32[64,576]{1,0:T(8,128)S(1)} %get-tuple-element.11) | data formatting | bytes 294912

commit v3 on v2

--- a/solution.py
+++ b/solution.py
@@ -197,19 +197,19 @@
 
     for n in range(4):
         loads[n].wait()
-        lax.fori_loop(n * (quarter // 512), (n + 1) * (quarter // 512), reorder, 0)
+        lax.fori_loop(n * (quarter // 512), (n + 1) * (quarter // 512), reorder, 0, unroll=True)
 
     def make_tile(i, carry):
         pair = jnp.concatenate(
             [spread[pl.ds(2 * i, 64, stride=height), :], spread[pl.ds(2 * i + 1, 64, stride=height), :]], axis=0)
-        tile = pair.T
-        tiles[i + 1, 0] = tile[:64].astype(BF16)
-        tiles[i + 1, 1] = tile[64:].astype(BF16)
-        west_out[pl.ds(i, 1), :] = tile[:1]
-        east_out[pl.ds(i, 1), :] = tile[127:]
-        return carry
-
-    lax.fori_loop(0, pairs, make_tile, 0, unroll=2)
+        tile = pair.astype(BF16).T
+        tiles[i + 1, 0] = tile[:64]
+        tiles[i + 1, 1] = tile[64:]
+        west_out[pl.ds(i, 1), :] = tile[:16].astype(F32)[:1]
+        east_out[pl.ds(i, 1), :] = tile[112:].astype(F32)[15:]
+        return carry
+
+    lax.fori_loop(0, pairs, make_tile, 0, unroll=8)
 
     pl.semaphore_wait(barrier, greeted)
     copies = []
@@ -256,7 +256,7 @@
             place(i, w, 0, 64, value)
         return carry
 
-    lax.fori_loop(0, pairs, lay, 0, unroll=2)
+    lax.fori_loop(0, pairs, lay, 0, unroll=4)
 
     for load in loads[4:]:
         load.wait()
@@ -269,7 +269,7 @@
         slope[at, :] = logistic * (1.0 + up * (1.0 - logistic))
         return carry
 
-    lax.fori_loop(0, chunks, activate, 0)
+    lax.fori_loop(0, chunks, activate, 0, unroll=2)
 
     def block(tap):
         return conv_ref[:, 64 * tap : 64 * tap + 64]
@@ -305,7 +305,7 @@
             place(i, w, low, low + 16, block)
         return carry
 
-    lax.fori_loop(0, pairs, mend, 0, unroll=2)
+    lax.fori_loop(0, pairs, mend, 0, unroll=4)
 
     def halo_windows(slot, corner):
         even, odd = tiles[slot, 0].astype(F32), tiles[slot, 1].astype(F32)
@@ -404,13 +404,21 @@
             conv_out[32 + at : 32 + at + spare, 512:] = line[:, 64:]
 
 
+def deliver_kernel(*refs):
+    copies = [pltpu.make_async_copy(refs[n], refs[3 + n], refs[6].at[n]) for n in range(3)]
+    for copy in copies:
+        copy.start()
+    for copy in copies:
+        copy.wait()
+
+
 def section(scale, coarse, cotangent, tconv, conv):
     cells = coarse.shape[0]
     pairs = cells // 64
     members, length = 2 * lax.axis_size("lat"), lax.axis_size("lon") // 4
     chunk = 272 // members
     vmem, hbm = pl.BlockSpec(memory_space=pltpu.VMEM), pl.BlockSpec(memory_space=pltpu.HBM)
-    return pl.pallas_call(
+    results = pl.pallas_call(
         functools.partial(section_kernel, scale),
         out_shape=(pltpu.VMEM((cells, 128), BF16), pltpu.VMEM((256, 128), F32), pltpu.VMEM(conv.shape, F32)),
         in_specs=[hbm] * 4,
@@ -442,6 +450,14 @@
         compiler_params=pltpu.CompilerParams(collective_id=0, has_side_effects=True, vmem_limit_bytes=VMEM_LIMIT),
         name="section",
     )(*(pltpu.with_memory_space_constraint(x, pltpu.HBM) for x in (coarse, cotangent, tconv, conv)))
+    return pl.pallas_call(
+        deliver_kernel,
+        out_shape=tuple(pltpu.HBM(x.shape, x.dtype) for x in results),
+        in_specs=[vmem] * 3,
+        out_specs=(hbm,) * 3,
+        scratch_shapes=[pltpu.SemaphoreType.DMA((3,))],
+        name="deliver",
+    )(*(pltpu.with_memory_space_constraint(x, pltpu.VMEM) for x in results))
 
 
 def per_device(coarse_field, cotangent, tconv_weight, conv_weight):

time: 40.6 us -> 38.6 us (0.951)
  local copies, waits for them, and re-layouts: 2.12 us -> 0 us
    unnamed x3 -> x0, local copies, waits for them, and re-layouts: 2.12 us -> none
    pallas_call x0 -> x1, Pallas kernels: none -> 0.91 us  [section(): pl.pallas_call(deliver_kernel, out_shape=tuple((pltpu.HBM(x.shape, x.dtyp...]
    pallas_call x1, Pallas kernels: 37.7 us -> 36.9 us  [section(): pl.pallas_call(functools.partial(section_kernel, scale), out_shape=(pltpu...]
where the time goes in v3:
time: 38.6 us; the launch traced here: 38.5 us
  Pallas kernels  37.8 us (98%)
  between operations  0.64 us (2%)
    pallas_call x1, Pallas kernels, section(): pl.pallas_call(functools.partial(section_kernel, scale), out_shape=(pltpu...  36.9 us
    pallas_call x1, Pallas kernels, section(): pl.pallas_call(deliver_kernel, out_shape=tuple((pltpu.HBM(x.shape, x.dtyp...  0.91 us

profile of v3, /device:TPU:1, one launch (start us, length us, event | category | flops | bytes accessed | tf_op | source)
XLA Modules:
  0.0 38.5 jit_solution(4941219834347657933)
XLA Ops:
  0.6 36.9 %section.1 = (bf16[2048,128]{1,0:T(8,128)(2,1)S(1)}, f32[256,128]{1,0:T(8,128)S(1)}, f32[64,576]{1,0:T(8,128)S(1)}) custom-call(bf16[2048,128]{1,0:T(8,128)(2,1)} %bitcast.10, bf16[4096,128]{1,0:T(8,128)(2,1)} %bitcast.9, bf16[256,128]{1,0:T(8,128)(2,1)} %bitcast.11, bf16[64,576]{1,0:T(8,128)(2,1)} %conv_hbm.1), custom_call_target="tpu_custom_call" | custom-call | tf_op jit(solution)/shard_map/section/pallas_call | solution.py:421
  37.6 0.9 %deliver.1 = (bf16[2048,128]{1,0:T(8,128)(2,1)}, f32[256,128]{1,0:T(8,128)}, f32[64,576]{1,0:T(8,128)}) custom-call(bf16[2048,128]{1,0:T(8,128)(2,1)S(1)} %get-tuple-element.9.refs_0_, f32[256,128]{1,0:T(8,128)S(1)} %get-tuple-element.10.refs_1_, f32[64,576]{1,0:T(8,128)S(1)} %get-tuple-element.11.refs_2_), custom_call_target="tpu_custom_call" | custom-call | tf_op jit(solution)/shard_map/deliver/pallas_call | solution.py:453

commit v4 on v3

--- a/solution.py
+++ b/solution.py
@@ -35,13 +35,14 @@
                             yield source, window, half, p, q, 3 * (a + 1) + b + 1
 
 
-def pole_blocks():
+def halo_blocks(side, polar):
+    half = side if polar else 1 - side
+    step = (2 * side - 1) if polar else (1 - 2 * side)
     for window in range(4):
-        for half in range(2):
-            for q in range(2):
-                b = col_step(window, q)
-                if b is not None:
-                    yield window, half, half, q, 3 * (2 * half) + b + 1
+        for q in range(2):
+            b = col_step(window, q)
+            if b is not None:
+                yield window, half, side, q, 3 * (step + 1) + b + 1
 
 
 def across(a, b):
@@ -50,14 +51,6 @@
 
 def times(a, b):
     return jnp.dot(a, b, preferred_element_type=F32)
-
-
-def each(low, high, act):
-    def step(n, carry):
-        act(n)
-        return carry
-
-    lax.fori_loop(low, high, step, 0)
 
 
 class Sum:
@@ -72,14 +65,16 @@
         self.near = lon - self.far * self.side
         self.z, self.core = self.near // 2, self.near % 2
         self.mine = self.far * self.lats + self.lat
+        self.far_first = sorted(
+            range(1, self.members),
+            key=lambda d: abs(2 * (d % self.lats) - self.lats) - 4 * (d // self.lats))
 
     def other(self):
         return {"lat": self.lat, "lon": self.far * self.side + self.z * 2 + 1 - self.core}
 
     def member(self, d):
-        flip = d >= self.lats
-        lat = self.lat + jnp.where(flip, d - self.lats, d)
-        return jnp.where(lat >= self.lats, lat - self.lats, lat), jnp.where(flip, 1 - self.far, self.far)
+        lat = self.lat + d % self.lats
+        return jnp.where(lat >= self.lats, lat - self.lats, lat), (1 - self.far if d >= self.lats else self.far)
 
     def plane(self, d):
         lat, far = self.member(d)
@@ -100,8 +95,10 @@
             pl.semaphore_signal(barrier, inc=1, device_id=peer, device_id_type=MESH)
 
         signal(self.other())
-        each(1, self.members, lambda d: signal(self.plane(d)))
-        each(1, self.length, lambda e: signal(self.line(e)))
+        for d in self.far_first:
+            signal(self.plane(d))
+        for e in range(1, self.length):
+            signal(self.line(e))
         return self.members + self.length - 1
 
     def all_of(self, phase):
@@ -120,7 +117,8 @@
             lat, far = self.member(d)
             self.copy(self.half.at[far * self.lats + lat], self.seen.at[d], 1, self.plane(d)).start()
 
-        each(1, self.members, send)
+        for d in self.far_first:
+            send(d)
 
     def pass_on(self):
         self.all_of(1).wait_recv()
@@ -128,7 +126,8 @@
         for d in range(1, self.members):
             total = total + self.seen[d]
         self.along[self.z] = total
-        each(1, self.length, lambda e: self.copy(self.along.at[self.z], self.along.at[self.z], 2, self.line(e)).start())
+        for e in sorted(range(1, self.length), key=lambda e: abs(2 * e - self.length)):
+            self.copy(self.along.at[self.z], self.along.at[self.z], 2, self.line(e)).start()
 
     def give_back(self):
         self.all_of(2).wait_recv()
@@ -137,7 +136,8 @@
             total = total + self.along[z]
         self.final[self.core, self.mine] = total * self.scale
         at = self.final.at[self.core, self.mine]
-        each(1, self.members, lambda d: self.copy(at, at, 3, self.plane(d)).start())
+        for d in self.far_first:
+            self.copy(at, at, 3, self.plane(d)).start()
 
     def bring_home(self):
         self.all_of(3).wait_recv()
@@ -152,8 +152,8 @@
 def section_kernel(
     scale, coarse_hbm, cot_hbm, tconv_hbm, conv_hbm, out_ref, taps_out, conv_out,
     coarse_ref, cot_ref, tconv_ref, conv_ref,
-    spread, tiles, west_out, east_out, west_in, east_in, patches, act_t, slope, pre, pre_t, weights, pole_weights,
-    pole_patches, pole_extra, pole_sums, send_sem, recv_sem, load_sem,
+    spread, tiles, west_out, east_out, west_in, east_in, patches, act_t, slope, pre, pre_t, weights, half_grad, half_sums, halo_weights,
+    halo_patches, send_sem, recv_sem, load_sem,
     shares, half, arrived, seen, along, final, sum_send, sum_recv,
 ):
     pairs = coarse_ref.shape[0] // 64
@@ -257,6 +257,9 @@
         return carry
 
     lax.fori_loop(0, pairs, lay, 0, unroll=4)
+    for w in range(4):
+        patches[64:128, 256 * w + 192 : 256 * w + 256] = jnp.zeros((64, 64), BF16)
+        patches[pairs * 64 : pairs * 64 + 64, 256 * w + 128 : 256 * w + 192] = jnp.zeros((64, 64), BF16)
 
     for load in loads[4:]:
         load.wait()
@@ -280,14 +283,24 @@
         line = [block(places[s, w, h, p, q]) if (s, w, h, p, q) in places else none for p in range(2) for q in range(2)]
         at = w * 256 + s * 128 + h * 64
         weights[at : at + 64, :] = jnp.concatenate(line, axis=1)
-    places = {(w, h, p, q): t for w, h, p, q, t in pole_blocks()}
-    for w, h in [(w, h) for w in range(4) for h in range(2)]:
-        line = [block(places[w, h, p, q]) if (w, h, p, q) in places else none for p in range(2) for q in range(2)]
-        at = w * 128 + h * 64
-        pole_weights[at : at + 64, :] = jnp.concatenate(line, axis=1)
-
-    pole_extra[...] = jnp.zeros_like(pole_extra)
-    pole_sums[...] = jnp.zeros_like(pole_sums)
+    def weigh_halo(side, polar):
+        places = {(w, h, p, q): t for w, h, p, q, t in halo_blocks(side, polar)}
+        for w, h in [(w, h) for w in range(4) for h in range(2)]:
+            line = [block(places[w, h, p, q]) if (w, h, p, q) in places else none for p in range(2) for q in range(2)]
+            at = w * 128 + h * 64
+            halo_weights[side, at : at + 64, :] = jnp.concatenate(line, axis=1)
+
+    at_pole = (at_north, at_south)
+    for side in range(2):
+        pl.when(at_pole[side])(lambda side=side: weigh_halo(side, True))
+        pl.when(jnp.logical_not(at_pole[side]))(lambda side=side: weigh_halo(side, False))
+    halo_patches[...] = jnp.zeros_like(halo_patches)
+
+    last = pairs * 64
+    for n in range(chunks):
+        half_grad[n * 256 : n * 256 + 256, :] = times(patches[n * 256 + 64 : n * 256 + 320, :512], weights[:512, :])
+    for w in range(2):
+        half_sums[w] = times(act_t[...], patches[64 : last + 64, 256 * w : 256 * w + 256])
 
     for landed, source in enumerate(
         (tiles.at[0], tiles.at[0], east_in.at[head], east_in.at[head], west_in.at[head],
@@ -313,37 +326,17 @@
 
     north = halo_windows(0, jnp.where(at_north, 0, 7))
     south = halo_windows(pairs + 1, jnp.where(at_south, pairs + 15, pairs + 8))
-    last = pairs * 64
     for w in range(4):
-        patches[64:128, 256 * w + 192 : 256 * w + 256] = jnp.where(at_north, 0.0, north[w][:, 64:]).astype(BF16)
-        patches[last : last + 64, 256 * w + 128 : 256 * w + 192] = jnp.where(at_south, 0.0, south[w][:, :64]).astype(BF16)
-
-    lane = lax.broadcasted_iota(jnp.int32, (64, 128), 1)
-    blank = jnp.zeros((64, 128), BF16)
-
-    @pl.when(at_north)
-    def _():
-        for w in range(4):
-            pole_patches[:64, 128 * w : 128 * w + 128] = jnp.where(lane < 64, north[w], 0.0).astype(BF16)
-            pole_patches[64:, 128 * w : 128 * w + 128] = blank
-        pole_extra[0] = times(pole_patches[...], pole_weights[...])
-        pole_sums[...] = times(act_t[:, :128], pole_patches[...])
-
-    @pl.when(at_south)
-    def _():
-        for w in range(4):
-            pole_patches[:64, 128 * w : 128 * w + 128] = blank
-            pole_patches[64:, 128 * w : 128 * w + 128] = jnp.where(lane < 64, 0.0, south[w]).astype(BF16)
-        pole_extra[1] = times(pole_patches[...], pole_weights[...])
-        pole_sums[...] = times(act_t[:, last - 128 :], pole_patches[...])
+        halo_patches[0, :64, 128 * w : 128 * w + 128] = north[w].astype(BF16)
+        halo_patches[1, 64:, 128 * w : 128 * w + 128] = south[w].astype(BF16)
 
     for n in range(chunks):
         at = slice(n * 256, n * 256 + 256)
-        grad = times(patches[n * 256 + 64 : n * 256 + 320, :], weights[...])
+        grad = half_grad[at, :] + times(patches[n * 256 + 64 : n * 256 + 320, 512:], weights[512:, :])
         if n == 0:
-            grad = jnp.concatenate([grad[:128] + pole_extra[0], grad[128:]], axis=0)
+            grad = jnp.concatenate([grad[:128] + times(halo_patches[0], halo_weights[0]), grad[128:]], axis=0)
         if n == chunks - 1:
-            grad = jnp.concatenate([grad[:128], grad[128:] + pole_extra[1]], axis=0)
+            grad = jnp.concatenate([grad[:128], grad[128:] + times(halo_patches[1], halo_weights[1])], axis=0)
         rounded = (grad * slope[at, :]).astype(BF16)
         pre[at, :] = rounded
         pre_t[:, at] = rounded.T
@@ -360,14 +353,18 @@
         found[tap] = value if tap not in found else found[tap] + value
 
     for w in range(4):
-        grads = times(act_t[...], patches[64 : last + 64, 256 * w : 256 * w + 256])
+        grads = half_sums[w] if w < 2 else times(act_t[...], patches[64 : last + 64, 256 * w : 256 * w + 256])
         for s, ww, h, p, q, t in window_blocks():
             if ww == w:
                 at, col = 128 * p + 64 * q, s * 128 + h * 64
                 add(t, grads[at : at + 64, col : col + 64])
-    for w, h, p, q, t in pole_blocks():
-        at, col = 128 * p + 64 * q, w * 128 + h * 64
-        add(t, pole_sums[at : at + 64, col : col + 64])
+    for side, cells in ((0, slice(0, 128)), (1, slice(last - 128, last))):
+        grads = times(act_t[:, cells], halo_patches[side])
+        for polar in (False, True):
+            for w, h, p, q, t in halo_blocks(side, polar):
+                at, col = 128 * p + 64 * q, w * 128 + h * 64
+                part = grads[at : at + 64, col : col + 64]
+                add(t, jnp.where(at_pole[side], part, 0.0) if polar else jnp.where(at_pole[side], 0.0, part))
     for b in range(4):
         both = jnp.concatenate([found[2 * b], found[2 * b + 1]], axis=0).T
         for m in range(members):
@@ -436,10 +433,10 @@
             pltpu.VMEM((cells, 256), BF16),
             pltpu.VMEM((256, cells), BF16),
             pltpu.VMEM((1024, 256), BF16),
-            pltpu.VMEM((512, 256), BF16),
-            pltpu.VMEM((128, 512), BF16),
-            pltpu.VMEM((2, 128, 256), F32),
-            pltpu.VMEM((256, 512), F32),
+            pltpu.VMEM((cells, 256), F32),
+            pltpu.VMEM((2, 256, 256), F32),
+            pltpu.VMEM((2, 512, 256), BF16),
+            pltpu.VMEM((2, 128, 512), BF16),
             pltpu.SemaphoreType.DMA((8,)), pltpu.SemaphoreType.DMA((8,)), pltpu.SemaphoreType.DMA((7,)),
             pltpu.VMEM((2, members, chunk, 128), F32),
             pltpu.VMEM((members, chunk, 128), F32), pltpu.VMEM((members, chunk, 128), F32),

time: 38.6 us -> 36.6 us (0.948)
  Pallas kernels: 37.8 us -> 35.9 us
    pallas_call x1, Pallas kernels: 36.9 us -> 35 us  [section(): pl.pallas_call(functools.partial(section_kernel, scale), out_shape=(pltpu...]
where the time goes in v4:
time: 36.6 us; the launch traced here: 36.5 us
  Pallas kernels  35.9 us (98%)
  between operations  0.64 us (2%)
    pallas_call x1, Pallas kernels, section(): pl.pallas_call(functools.partial(section_kernel, scale), out_shape=(pltpu...  35 us
    pallas_call x1, Pallas kernels, section(): pl.pallas_call(deliver_kernel, out_shape=tuple((pltpu.HBM(x.shape, x.dtyp...  0.91 us

profile of v4, /device:TPU:1, one launch (start us, length us, event | category | flops | bytes accessed | tf_op | source)
XLA Modules:
  0.0 36.5 jit_solution(9792064601609491975)
XLA Ops:
  0.6 35.0 %section.1 = (bf16[2048,128]{1,0:T(8,128)(2,1)S(1)}, f32[256,128]{1,0:T(8,128)S(1)}, f32[64,576]{1,0:T(8,128)S(1)}) custom-call(bf16[2048,128]{1,0:T(8,128)(2,1)} %bitcast.10, bf16[4096,128]{1,0:T(8,128)(2,1)} %bitcast.9, bf16[256,128]{1,0:T(8,128)(2,1)} %bitcast.11, bf16[64,576]{1,0:T(8,128)(2,1)} %conv_hbm.1), custom_call_target="tpu_custom_call" | custom-call | tf_op jit(solution)/shard_map/section/pallas_call | solution.py:418
  35.6 0.9 %deliver.1 = (bf16[2048,128]{1,0:T(8,128)(2,1)}, f32[256,128]{1,0:T(8,128)}, f32[64,576]{1,0:T(8,128)}) custom-call(bf16[2048,128]{1,0:T(8,128)(2,1)S(1)} %get-tuple-element.9.refs_0_, f32[256,128]{1,0:T(8,128)S(1)} %get-tuple-element.10.refs_1_, f32[64,576]{1,0:T(8,128)S(1)} %get-tuple-element.11.refs_2_), custom_call_target="tpu_custom_call" | custom-call | tf_op jit(solution)/shard_map/deliver/pallas_call | solution.py:450

commit v5 on v4

--- a/solution.py
+++ b/solution.py
@@ -68,6 +68,7 @@
         self.far_first = sorted(
             range(1, self.members),
             key=lambda d: abs(2 * (d % self.lats) - self.lats) - 4 * (d // self.lats))
+        self.both_cores = [(turn, d) for d in self.far_first for turn in range(2)] + [(1, 0)]
 
     def other(self):
         return {"lat": self.lat, "lon": self.far * self.side + self.z * 2 + 1 - self.core}
@@ -76,9 +77,10 @@
         lat = self.lat + d % self.lats
         return jnp.where(lat >= self.lats, lat - self.lats, lat), (1 - self.far if d >= self.lats else self.far)
 
-    def plane(self, d):
+    def plane(self, d, turn=0):
         lat, far = self.member(d)
-        return {"lat": lat, "lon": far * self.side + self.near}
+        core = 1 - self.core if turn else self.core
+        return {"lat": lat, "lon": far * self.side + self.z * 2 + core}
 
     def line(self, e):
         z = self.z + e
@@ -94,36 +96,28 @@
         def signal(peer):
             pl.semaphore_signal(barrier, inc=1, device_id=peer, device_id_type=MESH)
 
-        signal(self.other())
-        for d in self.far_first:
-            signal(self.plane(d))
+        for turn, d in self.both_cores:
+            signal(self.plane(d, turn))
         for e in range(1, self.length):
             signal(self.line(e))
-        return self.members + self.length - 1
+        return 2 * self.members + self.length - 2
 
     def all_of(self, phase):
-        part = (self.arrived, self.seen.at[pl.ds(1, self.members - 1)], self.along.at[pl.ds(1, self.length - 1)],
-                self.seen.at[pl.ds(1, self.members - 1)], self.arrived)[phase]
+        part = (self.arrived, self.seen.at[pl.ds(1, 2 * self.members - 1)], self.along.at[pl.ds(1, self.length - 1)],
+                self.seen.at[pl.ds(1, 2 * self.members - 1)], self.arrived)[phase]
         return self.copy(part, part, phase, self.other())
 
-    def start(self):
-        self.copy(self.source.at[1 - self.core], self.arrived, 0, self.other()).start()
-
     def scatter(self):
-        self.all_of(0).wait_recv()
-        self.half[...] = self.source[self.core] + self.arrived[...]
-
-        def send(d):
+        for turn, d in self.both_cores:
             lat, far = self.member(d)
-            self.copy(self.half.at[far * self.lats + lat], self.seen.at[d], 1, self.plane(d)).start()
-
-        for d in self.far_first:
-            send(d)
+            core = 1 - self.core if turn else self.core
+            self.copy(self.source.at[core, far * self.lats + lat], self.seen.at[turn * self.members + d], 1,
+                      self.plane(d, turn)).start()
 
     def pass_on(self):
         self.all_of(1).wait_recv()
-        total = self.half[self.mine]
-        for d in range(1, self.members):
+        total = self.source[self.core, self.mine]
+        for d in range(1, 2 * self.members):
             total = total + self.seen[d]
         self.along[self.z] = total
         for e in sorted(range(1, self.length), key=lambda e: abs(2 * e - self.length)):
@@ -136,16 +130,14 @@
             total = total + self.along[z]
         self.final[self.core, self.mine] = total * self.scale
         at = self.final.at[self.core, self.mine]
-        for d in self.far_first:
-            self.copy(at, at, 3, self.plane(d)).start()
+        for turn, d in self.both_cores:
+            self.copy(at, at, 3, self.plane(d, turn)).start()
 
     def bring_home(self):
         self.all_of(3).wait_recv()
-        self.copy(self.final.at[self.core], self.final.at[self.core], 4, self.other()).start()
 
     def end(self):
-        self.all_of(4).wait_recv()
-        for phase in range(5):
+        for phase in (1, 2, 3):
             self.all_of(phase).wait_send()
 
 
@@ -377,12 +369,11 @@
         for core in range(2):
             at = 16 * core + spare * m
             shares[core, m, share:] = last_tap[at : at + spare]
-    total.start()
+    total.scatter()
 
     for n in range(chunks):
         at = slice(n * 256, n * 256 + 256)
         out_ref[at, :] = times(pre[at, :], tconv_ref[...]).astype(BF16)
-    total.scatter()
     total.pass_on()
     total.give_back()
     total.bring_home()
@@ -402,7 +393,11 @@
 
 
 def deliver_kernel(*refs):
-    copies = [pltpu.make_async_copy(refs[n], refs[3 + n], refs[6].at[n]) for n in range(3)]
+    copies = [pltpu.make_async_copy(refs[n], refs[3 + n], refs[6].at[n]) for n in (1, 2)]
+    quarter = refs[0].shape[0] // 4
+    for n in range(4):
+        at = pl.ds(n * quarter, quarter)
+        copies.append(pltpu.make_async_copy(refs[0].at[at], refs[3].at[at], refs[6].at[3 + n]))
     for copy in copies:
         copy.start()
     for copy in copies:
@@ -440,7 +435,7 @@
             pltpu.SemaphoreType.DMA((8,)), pltpu.SemaphoreType.DMA((8,)), pltpu.SemaphoreType.DMA((7,)),
             pltpu.VMEM((2, members, chunk, 128), F32),
             pltpu.VMEM((members, chunk, 128), F32), pltpu.VMEM((members, chunk, 128), F32),
-            pltpu.VMEM((members, chunk, 128), F32), pltpu.VMEM((length, chunk, 128), F32),
+            pltpu.VMEM((2 * members, chunk, 128), F32), pltpu.VMEM((length, chunk, 128), F32),
             pltpu.VMEM((2, members, chunk, 128), F32),
             pltpu.SemaphoreType.DMA((5,)), pltpu.SemaphoreType.DMA((5,)),
         ],
@@ -452,7 +447,7 @@
         out_shape=tuple(pltpu.HBM(x.shape, x.dtype) for x in results),
         in_specs=[vmem] * 3,
         out_specs=(hbm,) * 3,
-        scratch_shapes=[pltpu.SemaphoreType.DMA((3,))],
+        scratch_shapes=[pltpu.SemaphoreType.DMA((7,))],
         name="deliver",
     )(*(pltpu.with_memory_space_constraint(x, pltpu.VMEM) for x in results))
 

time: 36.6 us -> 36.5 us (level)
  no operation moved by 1% of the time
where the time goes in v5:
time: 36.5 us; the launch traced here: 36.4 us
  Pallas kernels  35.8 us (98%)
  between operations  0.64 us (2%)
    pallas_call x1, Pallas kernels, section(): pl.pallas_call(functools.partial(section_kernel, scale), out_shape=(pltpu...  34.8 us
    pallas_call x1, Pallas kernels, section(): pl.pallas_call(deliver_kernel, out_shape=tuple((pltpu.HBM(x.shape, x.dtyp...  0.94 us

profile of v5, /device:TPU:1, one launch (start us, length us, event | category | flops | bytes accessed | tf_op | source)
XLA Modules:
  0.0 36.4 jit_solution(12662518794708227420)
XLA Ops:
  0.6 34.8 %section.1 = (bf16[2048,128]{1,0:T(8,128)(2,1)S(1)}, f32[256,128]{1,0:T(8,128)S(1)}, f32[64,576]{1,0:T(8,128)S(1)}) custom-call(bf16[2048,128]{1,0:T(8,128)(2,1)} %bitcast.10, bf16[4096,128]{1,0:T(8,128)(2,1)} %bitcast.9, bf16[256,128]{1,0:T(8,128)(2,1)} %bitcast.11, bf16[64,576]{1,0:T(8,128)(2,1)} %conv_hbm.1), custom_call_target="tpu_custom_call" | custom-call | tf_op jit(solution)/shard_map/section/pallas_call | solution.py:413
  35.5 0.9 %deliver.1 = (bf16[2048,128]{1,0:T(8,128)(2,1)}, f32[256,128]{1,0:T(8,128)}, f32[64,576]{1,0:T(8,128)}) custom-call(bf16[2048,128]{1,0:T(8,128)(2,1)S(1)} %get-tuple-element.9.refs_0_, f32[256,128]{1,0:T(8,128)S(1)} %get-tuple-element.10.refs_1_, f32[64,576]{1,0:T(8,128)S(1)} %get-tuple-element.11.refs_2_), custom_call_target="tpu_custom_call" | custom-call | tf_op jit(solution)/shard_map/deliver/pallas_call | solution.py:445

commit v6 on v5

--- a/solution.py
+++ b/solution.py
@@ -248,7 +248,7 @@
             place(i, w, 0, 64, value)
         return carry
 
-    lax.fori_loop(0, pairs, lay, 0, unroll=4)
+    lax.fori_loop(0, pairs, lay, 0, unroll=8)
     for w in range(4):
         patches[64:128, 256 * w + 192 : 256 * w + 256] = jnp.zeros((64, 64), BF16)
         patches[pairs * 64 : pairs * 64 + 64, 256 * w + 128 : 256 * w + 192] = jnp.zeros((64, 64), BF16)
@@ -264,7 +264,7 @@
         slope[at, :] = logistic * (1.0 + up * (1.0 - logistic))
         return carry
 
-    lax.fori_loop(0, chunks, activate, 0, unroll=2)
+    lax.fori_loop(0, chunks, activate, 0, unroll=4)
 
     def block(tap):
         return conv_ref[:, 64 * tap : 64 * tap + 64]
@@ -310,7 +310,7 @@
             place(i, w, low, low + 16, block)
         return carry
 
-    lax.fori_loop(0, pairs, mend, 0, unroll=4)
+    lax.fori_loop(0, pairs, mend, 0, unroll=16)
 
     def halo_windows(slot, corner):
         even, odd = tiles[slot, 0].astype(F32), tiles[slot, 1].astype(F32)

time: 36.5 us -> 36 us (0.986)
  Pallas kernels: 35.8 us -> 35.3 us
    pallas_call x1, Pallas kernels: 34.8 us -> 34.4 us  [section(): pl.pallas_call(functools.partial(section_kernel, scale), out_shape=(pltpu...]
where the time goes in v6:
time: 36 us; the launch traced here: 35.9 us
  Pallas kernels  35.3 us (98%)
  between operations  0.64 us (2%)
    pallas_call x1, Pallas kernels, section(): pl.pallas_call(functools.partial(section_kernel, scale), out_shape=(pltpu...  34.4 us
    pallas_call x1, Pallas kernels, section(): pl.pallas_call(deliver_kernel, out_shape=tuple((pltpu.HBM(x.shape, x.dtyp...  0.94 us

profile of v6, /device:TPU:1, one launch (start us, length us, event | category | flops | bytes accessed | tf_op | source)
XLA Modules:
  0.0 35.9 jit_solution(8517883824641936131)
XLA Ops:
  0.6 34.4 %section.1 = (bf16[2048,128]{1,0:T(8,128)(2,1)S(1)}, f32[256,128]{1,0:T(8,128)S(1)}, f32[64,576]{1,0:T(8,128)S(1)}) custom-call(bf16[2048,128]{1,0:T(8,128)(2,1)} %bitcast.10, bf16[4096,128]{1,0:T(8,128)(2,1)} %bitcast.9, bf16[256,128]{1,0:T(8,128)(2,1)} %bitcast.11, bf16[64,576]{1,0:T(8,128)(2,1)} %conv_hbm.1), custom_call_target="tpu_custom_call" | custom-call | tf_op jit(solution)/shard_map/section/pallas_call | solution.py:413
  35.0 0.9 %deliver.1 = (bf16[2048,128]{1,0:T(8,128)(2,1)}, f32[256,128]{1,0:T(8,128)}, f32[64,576]{1,0:T(8,128)}) custom-call(bf16[2048,128]{1,0:T(8,128)(2,1)S(1)} %get-tuple-element.9.refs_0_, f32[256,128]{1,0:T(8,128)S(1)} %get-tuple-element.10.refs_1_, f32[64,576]{1,0:T(8,128)S(1)} %get-tuple-element.11.refs_2_), custom_call_target="tpu_custom_call" | custom-call | tf_op jit(solution)/shard_map/deliver/pallas_call | solution.py:445
